TPU v7x, 512 devices: a whole 4x4x16 slice. The times are simulated.
512 devices in a mesh: dp: 32 (over z, core), ctx: 16 (over x, y).
Axes of the slice: x: 4, y: 4, z: 16, core: 2. Of those that a mesh axis runs over, the one named last changes fastest.
Arguments:
- queries: bfloat16 [65536, 2048], P(('dp', 'ctx')), may hold values from -120 to 120
- keys: bfloat16 [65536, 1024], P(('dp', 'ctx')), may hold values from -4 to 4
- values: bfloat16 [65536, 1024], P(('dp', 'ctx')), may hold values from -6 to 6
- grad_out: bfloat16 [65536, 2048], P(('dp', 'ctx')), may hold values from -6 to 6
- doc_lengths: int32 [128], replicated, may hold values from 1 to 1024, 65536 in all
Outputs:
- attended: bfloat16 [65536, 2048], P(('dp', 'ctx'))
- grad_queries: bfloat16 [65536, 2048], P(('dp', 'ctx'))
- grad_keys: bfloat16 [65536, 1024], P(('dp', 'ctx'))
- grad_values: bfloat16 [65536, 1024], P(('dp', 'ctx'))
Inputs may be any that keep to these rules, and one draw needn't show every extreme that they name: doc_lengths lists 128 documents that fill all 65536 tokens in order; the longest has exactly 1024 tokens.
All inputs are finite; a program needn't handle non-finite values.
Results may differ from a plain program's by a relative error of at most 0.024.
Values may be sent and summed in bfloat16 or wider, within the bound.
No kernel may reach another device: no remote copies, remote signals or barrier semaphores. Data moves between devices by JAX's collectives and lax.ppermute only.
A program may use at most 128 MiB of HBM per device.

v0:
```python
from functools import reduce

import jax
import jax.numpy as jnp
from jax import lax
from jax.sharding import PartitionSpec as P

HEADS = 16
KV_HEADS = 8
HD = 128


q_scale = 144.0 ** (-0.5)
far_below = -1e30


def passed_along(array, axis, by):
    devices = lax.axis_size(axis)
    pairs = [(i, i + by) for i in range(devices) if 0 <= i + by < devices]
    return lax.ppermute(array, axis, pairs)


def doc_ids(doc_lengths, positions):
    ends = jnp.cumsum(doc_lengths)
    found = jnp.sum((ends[None, :] <= positions[:, None]).astype(jnp.int32), axis=1)
    return jnp.where(positions >= 0, found, -1)


def score_piece(q_blk, k_sub, allowed):
    scores = jnp.einsum("qhd,khd->hqk", q_blk, k_sub, preferred_element_type=jnp.float32) * q_scale
    return jnp.where(allowed[None], scores, far_below)


def rows_by_keys(left, k_sub):
    return jnp.einsum("hqk,khd->qhd", left, k_sub, preferred_element_type=jnp.float32)


def keys_by_rows(left, q_blk):
    return jnp.einsum("hqk,qhd->khd", left, q_blk, preferred_element_type=jnp.float32)


def pair_products(d_blk, v_sub):
    return jnp.einsum("qhd,khd->hqk", d_blk, v_sub, preferred_element_type=jnp.float32)


def attend_block(q_blk, d_blk, k_subs, v_subs, masks):
    active_flags = [jnp.any(allowed) for allowed in masks]
    scores = [score_piece(q_blk, k_sub, allowed) for k_sub, allowed in zip(k_subs, masks)]
    highest = reduce(jnp.maximum, [jnp.max(piece, axis=2, keepdims=True) for piece in scores])
    summed = reduce(
        jnp.add, [jnp.sum(jnp.exp(piece - highest), axis=2, keepdims=True) for piece in scores]
    )
    log_total = highest + jnp.log(summed)
    weights = [jnp.exp(piece - log_total) for piece in scores]
    weights_b = [weight.astype(jnp.bfloat16) for weight in weights]
    mixture = reduce(
        jnp.add, [rows_by_keys(weight, v_sub) for weight, v_sub in zip(weights_b, v_subs)]
    )
    attended = mixture.astype(jnp.bfloat16)
    row_delta = jnp.sum(
        d_blk.astype(jnp.float32) * mixture.astype(jnp.bfloat16).astype(jnp.float32), axis=2
    )
    delta_cols = jnp.transpose(row_delta)[:, :, None]
    dscores_b = []
    for weight, v_sub, active in zip(weights, v_subs, active_flags):
        dprob = pair_products(d_blk, v_sub)
        dscores_b.append((weight * (dprob - delta_cols)).astype(jnp.bfloat16))
    grad_q = (
        reduce(jnp.add, [rows_by_keys(dscore, k_sub) for dscore, k_sub in zip(dscores_b, k_subs)])
        * q_scale
    )
    grad_k = [keys_by_rows(dscore, q_blk) * q_scale for dscore in dscores_b]
    grad_v = [keys_by_rows(weight, d_blk) for weight in weights_b]
    return (attended, grad_q, grad_k, grad_v)


def on_device(queries, keys, values, grad_out, doc_lengths):
    lane_count = lax.axis_size("ctx")
    tok_rows = queries.shape[0]
    row_len = tok_rows * lane_count
    reach_len = row_len // 2
    block_len = row_len // 4
    local_heads = HEADS // lane_count
    group_size = HEADS // KV_HEADS
    key_copies = jnp.repeat(keys.reshape(tok_rows, KV_HEADS, HD), group_size, axis=1).reshape(
        tok_rows, HEADS * HD
    )
    value_copies = jnp.repeat(values.reshape(tok_rows, KV_HEADS, HD), group_size, axis=1).reshape(
        tok_rows, HEADS * HD
    )
    query_rows, key_rows, value_rows, output_grads = (
        lax.all_to_all(queries, "ctx", split_axis=1, concat_axis=0, tiled=True),
        lax.all_to_all(key_copies, "ctx", split_axis=1, concat_axis=0, tiled=True),
        lax.all_to_all(value_copies, "ctx", split_axis=1, concat_axis=0, tiled=True),
        lax.all_to_all(grad_out, "ctx", split_axis=1, concat_axis=0, tiled=True),
    )
    key_rows = key_rows.reshape(row_len, local_heads, HD)
    value_rows = value_rows.reshape(row_len, local_heads, HD)
    query_rows = query_rows.reshape(row_len, local_heads, HD)
    output_grads = output_grads.reshape(row_len, local_heads, HD)
    prev_keys, prev_values = passed_along((key_rows, value_rows), "dp", 1)
    prev_keys = prev_keys[row_len - reach_len :]
    prev_values = prev_values[row_len - reach_len :]
    key_all = jnp.concatenate([prev_keys, key_rows], axis=0)
    value_all = jnp.concatenate([prev_values, value_rows], axis=0)
    row_start = lax.axis_index("dp") * row_len
    positions = row_start - reach_len + jnp.arange(reach_len + row_len, dtype=jnp.int32)
    doc_of = doc_ids(doc_lengths, positions)
    attended_parts = []
    grad_q_parts = []
    key_grads = jnp.zeros((reach_len + row_len, local_heads, HD), jnp.float32)
    value_grads = jnp.zeros((reach_len + row_len, local_heads, HD), jnp.float32)
    for block_index in range(4):
        own_start = block_index * block_len
        q_blk = query_rows[own_start : own_start + block_len]
        d_blk = output_grads[own_start : own_start + block_len]
        q_ids = doc_of[reach_len + own_start : reach_len + own_start + block_len]
        q_pos = positions[reach_len + own_start : reach_len + own_start + block_len]
        k_subs = []
        v_subs = []
        masks = []
        for sub_index in range(3):
            key_start = own_start + sub_index * block_len
            k_subs.append(key_all[key_start : key_start + block_len])
            v_subs.append(value_all[key_start : key_start + block_len])
            k_ids = doc_of[key_start : key_start + block_len]
            k_pos = positions[key_start : key_start + block_len]
            masks.append((q_ids[:, None] == k_ids[None, :]) & (k_pos[None, :] <= q_pos[:, None]))
        attended, grad_q, grad_k, grad_v = attend_block(q_blk, d_blk, k_subs, v_subs, masks)
        attended_parts.append(attended)
        grad_q_parts.append(grad_q)
        for sub_index in range(3):
            key_start = own_start + sub_index * block_len
            key_grads = key_grads.at[key_start : key_start + block_len].add(grad_k[sub_index])
            value_grads = value_grads.at[key_start : key_start + block_len].add(grad_v[sub_index])
    attended_rows = jnp.concatenate(attended_parts, axis=0).reshape(row_len, local_heads * HD)
    grad_q_rows = (
        jnp.concatenate(grad_q_parts, axis=0)
        .astype(jnp.bfloat16)
        .reshape(row_len, local_heads * HD)
    )
    sent_keys, sent_values = passed_along(
        (key_grads[:reach_len], value_grads[:reach_len]), "dp", -1
    )
    own_key_grads = key_grads[reach_len:].at[row_len - reach_len :].add(sent_keys)
    own_value_grads = value_grads[reach_len:].at[row_len - reach_len :].add(sent_values)
    attended_out, grad_queries = (
        lax.all_to_all(attended_rows, "ctx", split_axis=0, concat_axis=1, tiled=True),
        lax.all_to_all(grad_q_rows, "ctx", split_axis=0, concat_axis=1, tiled=True),
    )
    back_keys, back_values = (
        lax.all_to_all(
            own_key_grads.reshape(row_len, local_heads * HD),
            "ctx",
            split_axis=0,
            concat_axis=1,
            tiled=True,
        ),
        lax.all_to_all(
            own_value_grads.reshape(row_len, local_heads * HD),
            "ctx",
            split_axis=0,
            concat_axis=1,
            tiled=True,
        ),
    )
    grad_keys = (
        jnp.sum(back_keys.reshape(tok_rows, KV_HEADS, group_size, HD), axis=2)
        .reshape(tok_rows, KV_HEADS * HD)
        .astype(jnp.bfloat16)
    )
    grad_values = (
        jnp.sum(back_values.reshape(tok_rows, KV_HEADS, group_size, HD), axis=2)
        .reshape(tok_rows, KV_HEADS * HD)
        .astype(jnp.bfloat16)
    )
    return (attended_out, grad_queries, grad_keys, grad_values)


def solution(mesh):
    in_specs = (
        P(("dp", "ctx"), None),
        P(("dp", "ctx"), None),
        P(("dp", "ctx"), None),
        P(("dp", "ctx"), None),
        P(),
    )
    out_specs = (
        P(("dp", "ctx"), None),
        P(("dp", "ctx"), None),
        P(("dp", "ctx"), None),
        P(("dp", "ctx"), None),
    )
    return jax.shard_map(
        on_device, mesh=mesh, in_specs=in_specs, out_specs=out_specs, check_vma=False
    )
```

profile of v0, /device:TPU:32, one launch (start us, length us, event | category | flops | bytes accessed | tf_op | source)
XLA Modules:
  0.0 197.0 jit_solution(6814654371073003441)
XLA Ops:
  0.7 2.1 %copy.117 = bf16[128,2048]{0,1:T(8,128)(2,1)} copy(bf16[128,2048]{1,0:T(8,128)(2,1)} %param.57) | data formatting | bytes 1048576 | tf_op args[0]
  2.8 7.0 %all-to-all-start = ((bf16[128,16,128]{0,2,1:T(8,128)(2,1)}), bf16[128,16,128]{0,2,1:T(8,128)(2,1)S(1)}, u32[]{:S(2)}, u32[]{:S(2)}) async-start(bf16[128,16,128]{0,2,1:T(8,128)(2,1)} %bitcast.1), calls=%async_computation | async-start | bytes 1048576 | tf_op jit(solution)/shard_map/all_to_all | solution.py:92
  10.3 1.9 convert_reduce_fusion
  12.3 9.0 %all-to-all-done = bf16[128,16,128]{0,2,1:T(8,128)(2,1)S(1)} async-done(((bf16[128,16,128]{0,2,1:T(8,128)(2,1)}), bf16[128,16,128]{0,2,1:T(8,128)(2,1)S(1)}, u32[]{:S(2)}, u32[]{:S(2)}) %all-to-all-start) | async-done | bytes 524320 | tf_op jit(solution)/shard_map/all_to_all | solution.py:92
  21.3 0.9 broadcast_in_dim.24
  22.2 3.6 %all-to-all-start.1 = ((bf16[128,16,128]{2,0,1:T(8,128)(2,1)}), bf16[128,16,128]{2,0,1:T(8,128)(2,1)S(1)}, u32[]{:S(2)}, u32[]{:S(2)}) async-start(bf16[128,16,128]{2,0,1:T(8,128)(2,1)} %bitcast.4), calls=%async_computation.1 | async-start | bytes 1048576 | tf_op jit(solution)/shard_map/all_to_all | solution.py:93
  26.5 0.9 copy_bitcast_fusion.2
  28.1 7.9 %all-to-all-done.1 = bf16[128,16,128]{2,0,1:T(8,128)(2,1)S(1)} async-done(((bf16[128,16,128]{2,0,1:T(8,128)(2,1)}), bf16[128,16,128]{2,0,1:T(8,128)(2,1)S(1)}, u32[]{:S(2)}, u32[]{:S(2)}) %all-to-all-start.1) | async-done | bytes 524320 | tf_op jit(solution)/shard_map/all_to_all | solution.py:93
  36.1 4.2 %all-to-all-start.4 = ((bf16[128,16,128]{2,0,1:T(8,128)(2,1)}), bf16[128,16,128]{2,0,1:T(8,128)(2,1)}, u32[]{:S(2)}, u32[]{:S(2)}) async-start(bf16[128,16,128]{2,0,1:T(8,128)(2,1)} %copy_bitcast_fusion.2), calls=%async_computation.4 | async-start | bytes 1048576 | tf_op jit(solution)/shard_map/all_to_all | solution.py:95
  41.4 1.0 fusion.170
  42.4 1.9 fusion.172
  44.4 1.0 fusion.168
  45.4 5.1 %all-to-all-done.4 = bf16[128,16,128]{2,0,1:T(8,128)(2,1)} async-done(((bf16[128,16,128]{2,0,1:T(8,128)(2,1)}), bf16[128,16,128]{2,0,1:T(8,128)(2,1)}, u32[]{:S(2)}, u32[]{:S(2)}) %all-to-all-start.4) | async-done | bytes 524320 | tf_op jit(solution)/shard_map/all_to_all | solution.py:95
  50.4 0.9 broadcast_in_dim.26
  51.3 4.2 %all-to-all-start.2 = ((bf16[128,16,128]{2,0,1:T(8,128)(2,1)}), bf16[128,16,128]{2,0,1:T(8,128)(2,1)}, u32[]{:S(2)}, u32[]{:S(2)}) async-start(bf16[128,16,128]{2,0,1:T(8,128)(2,1)} %bitcast.553), calls=%async_computation.2 | async-start | bytes 1048576 | tf_op jit(solution)/shard_map/all_to_all | solution.py:94
  55.6 1.1 fusion.161
  56.8 2.0 %fusion.169 = (f32[512]{0:T(512)}, f32[512,512]{0,1:T(8,128)}) fusion(bf16[512,128]{1,0:T(8,128)(2,1)S(1)} %bitcast.525, bf16[512,128]{1,0:T(8,128)(2,1)S(1)} %bitcast.569, s32[512]{0:T(512)S(1)} %copy-done.48, s32[512]{0:T(512)S(1)} %copy-done.53, s32[512]{0:T(512)S(1)} %copy-done.51, s32[512]{0:T(512)S(1)} %copy-done.45), kind=kOutput, calls=%fused_computation.261 | convolution fusion | flops 68681216 | bytes 1320960 | tf_op jit(solution)/shard_map/qhd,khd->hqk/dot_general | solution.py:30
  58.8 6.9 %all-to-all-done.2 = bf16[128,16,128]{2,0,1:T(8,128)(2,1)} async-done(((bf16[128,16,128]{2,0,1:T(8,128)(2,1)}), bf16[128,16,128]{2,0,1:T(8,128)(2,1)}, u32[]{:S(2)}, u32[]{:S(2)}) %all-to-all-start.2) | async-done | bytes 524320 | tf_op jit(solution)/shard_map/all_to_all | solution.py:94
  65.7 1.2 fusion.164
  66.9 1.4 fusion.171
  69.5 1.0 fusion.127
  70.5 1.1 fusion.29
  71.6 1.1 fusion.28
  72.7 1.1 fusion.27
  75.4 1.0 fusion.126
  76.4 1.1 fusion.26
  77.5 1.1 fusion.25
  78.6 1.1 fusion.24
  79.7 1.7 copy.118
  81.4 1.9 collective-permute-start
  83.3 1.7 copy.121
  85.0 1.5 fusion.175
  86.5 4.2 %collective-permute-start.1 = (bf16[2048,1,128]{2,0,1:T(8,128)(2,1)}, bf16[2048,1,128]{2,0,1:T(8,128)(2,1)S(1)}, u32[]{:S(2)}, u32[]{:S(2)}) collective-permute-start(bf16[2048,1,128]{2,0,1:T(8,128)(2,1)} %bitcast.12), channel_id=1, source_target_pairs={{0,16},{16,32},{32,48},{48,64},{64,80},{80,96},{96,112},{112,128},... | collective-permute-start | bytes 1572872 | tf_op jit(solution)/shard_map/ppermute | solution.py:20
  94.0 1.3 fusion.178
  95.3 1.3 fusion.177
  98.5 1.3 fusion.174
  105.2 1.0 slice.893
  106.2 1.0 slice_bitcast_fusion
  107.2 1.0 fusion.128
  108.9 2.1 %collective-permute-start.3 = (f32[1024,1,128]{2,0,1:T(8,128)}, f32[1024,1,128]{2,0,1:T(8,128)}, u32[]{:S(2)}, u32[]{:S(2)}) collective-permute-start(f32[1024,1,128]{2,0,1:T(8,128)} %slice.893), channel_id=1, source_target_pairs={{16,0},{32,16},{48,32},{64,48},{80,64},{96,80},{112,96},{128,112},... | collective-permute-start | bytes 1572872 | tf_op jit(solution)/shard_map/ppermute | solution.py:20
  111.3 1.0 fusion.129
  117.3 1.2 fusion.160
  118.5 1.3 fusion.104
  119.8 1.3 fusion.105
  121.1 0.8 pad_maximum_fusion.1
  121.9 4.4 %all-to-all-start.5 = ((bf16[16,128,128]{2,1,0:T(8,128)(2,1)}), bf16[16,128,128]{2,1,0:T(8,128)(2,1)}, u32[]{:S(2)}, u32[]{:S(2)}) async-start(bf16[16,128,128]{2,1,0:T(8,128)(2,1)} %bitcast.552), calls=%async_computation.5 | async-start | bytes 1048576 | tf_op jit(solution)/shard_map/all_to_all | solution.py:149
  126.7 1.9 pad_maximum_fusion
  128.9 9.9 %all-to-all-done.5 = bf16[16,128,128]{2,1,0:T(8,128)(2,1)} async-done(((bf16[16,128,128]{2,1,0:T(8,128)(2,1)}), bf16[16,128,128]{2,1,0:T(8,128)(2,1)}, u32[]{:S(2)}, u32[]{:S(2)}) %all-to-all-start.5) | async-done | bytes 524320 | tf_op jit(solution)/shard_map/all_to_all | solution.py:149
  138.8 4.2 %all-to-all-start.3 = ((bf16[16,128,128]{2,1,0:T(8,128)(2,1)}), bf16[16,128,128]{2,1,0:T(8,128)(2,1)}, u32[]{:S(2)}, u32[]{:S(2)}) async-start(bf16[16,128,128]{2,1,0:T(8,128)(2,1)} %bitcast.551), calls=%async_computation.3 | async-start | bytes 1048576 | tf_op jit(solution)/shard_map/all_to_all | solution.py:148
  143.3 2.1 %fusion.123 = f32[2048,128]{1,0:T(8,128)} fusion(f32[2048,128]{1,0:T(8,128)} %slice_bitcast_fusion, f32[1024,1,128]{2,0,1:T(8,128)} %collective-permute-done.3, f32[3072,1,128]{2,0,1:T(8,128)} %copy-done.1), kind=kLoop, calls=%fused_computation.216 | loop fusion | flops 131072 | bytes 1572864 | tf_op jit(solution)/shard_map/scatter-add | solution.py:146
  145.4 8.6 %all-to-all-done.3 = bf16[16,128,128]{2,1,0:T(8,128)(2,1)} async-done(((bf16[16,128,128]{2,1,0:T(8,128)(2,1)}), bf16[16,128,128]{2,1,0:T(8,128)(2,1)}, u32[]{:S(2)}, u32[]{:S(2)}) %all-to-all-start.3) | async-done | bytes 524320 | tf_op jit(solution)/shard_map/all_to_all | solution.py:148
  154.0 4.3 %all-to-all-start.7 = ((f32[16,128,128]{2,1,0:T(8,128)}), f32[16,128,128]{2,1,0:T(8,128)}, u32[]{:S(2)}, u32[]{:S(2)}) async-start(f32[16,128,128]{2,1,0:T(8,128)} %bitcast.519), calls=%async_computation.7 | async-start | bytes 2097152 | tf_op jit(solution)/shard_map/all_to_all | solution.py:159
  158.7 1.9 collective-permute-start.2
  160.7 1.1 slice_bitcast_fusion.1
  161.7 5.6 %collective-permute-done.2 = f32[1024,1,128]{2,0,1:T(8,128)S(1)} collective-permute-done((f32[1024,1,128]{2,0,1:T(8,128)S(1)}, f32[1024,1,128]{2,0,1:T(8,128)S(1)}, u32[]{:S(2)}, u32[]{:S(2)}) %collective-permute-start.2) | collective-permute-done | bytes 524320 | tf_op jit(solution)/shard_map/ppermute | solution.py:20
  167.3 0.8 fusion.125
  168.2 4.9 %all-to-all-done.7 = f32[16,128,128]{2,1,0:T(8,128)} async-done(((f32[16,128,128]{2,1,0:T(8,128)}), f32[16,128,128]{2,1,0:T(8,128)}, u32[]{:S(2)}, u32[]{:S(2)}) %all-to-all-start.7) | async-done | bytes 1048608 | tf_op jit(solution)/shard_map/all_to_all | solution.py:159
  173.1 3.7 %all-to-all-start.6 = ((f32[16,128,128]{2,1,0:T(8,128)}), f32[16,128,128]{2,1,0:T(8,128)S(1)}, u32[]{:S(2)}, u32[]{:S(2)}) async-start(f32[16,128,128]{2,1,0:T(8,128)} %bitcast.96), calls=%async_computation.6 | async-start | bytes 2097152 | tf_op jit(solution)/shard_map/all_to_all | solution.py:152
  176.8 1.9 copy_bitcast_fusion
  178.7 1.9 copy_bitcast_fusion.1
  180.6 1.3 bitcast_reduce_fusion
  182.1 0.9 copy.142
  182.9 13.0 %all-to-all-done.6 = f32[16,128,128]{2,1,0:T(8,128)S(1)} async-done(((f32[16,128,128]{2,1,0:T(8,128)}), f32[16,128,128]{2,1,0:T(8,128)S(1)}, u32[]{:S(2)}, u32[]{:S(2)}) %all-to-all-start.6) | async-done | bytes 1048608 | tf_op jit(solution)/shard_map/all_to_all | solution.py:152
  196.2 0.9 copy.141
  (201 shorter events, 23.3 us)
Async XLA Ops:
  0.6 25.8 %copy-start = (bf16[128,2048]{1,0:T(8,128)(2,1)S(1)}, bf16[128,2048]{1,0:T(8,128)(2,1)}, u32[]{:S(2)}) copy-start(bf16[128,2048]{1,0:T(8,128)(2,1)} %param.60) | copy-start | bytes 1572868
  0.6 9.2 %copy-start.58 = (s32[128]{0:T(128)S(1)}, s32[128]{0:T(128)}, u32[]{:S(2)}) copy-start(s32[128]{0:T(128)} %param.61) | copy-start | bytes 1540
  0.7 11.5 %copy-start.33 = (bf16[128,1024]{1,0:T(8,128)(2,1)S(1)}, bf16[128,1024]{1,0:T(8,128)(2,1)}, u32[]{:S(2)}) copy-start(bf16[128,1024]{1,0:T(8,128)(2,1)} %param.58) | copy-start | bytes 786436
  0.7 11.6 %copy-start.34 = (bf16[128,1024]{1,0:T(8,128)(2,1)S(1)}, bf16[128,1024]{1,0:T(8,128)(2,1)}, u32[]{:S(2)}) copy-start(bf16[128,1024]{1,0:T(8,128)(2,1)} %param.59) | copy-start | bytes 786436
  2.8 18.5 %all-to-all-start = ((bf16[128,16,128]{0,2,1:T(8,128)(2,1)}), bf16[128,16,128]{0,2,1:T(8,128)(2,1)S(1)}, u32[]{:S(2)}, u32[]{:S(2)}) async-start(bf16[128,16,128]{0,2,1:T(8,128)(2,1)} %bitcast.1), calls=%async_computation | async-start | bytes 1048576 | tf_op jit(solution)/shard_map/all_to_all | solution.py:92
  22.2 13.8 %all-to-all-start.1 = ((bf16[128,16,128]{2,0,1:T(8,128)(2,1)}), bf16[128,16,128]{2,0,1:T(8,128)(2,1)S(1)}, u32[]{:S(2)}, u32[]{:S(2)}) async-start(bf16[128,16,128]{2,0,1:T(8,128)(2,1)} %bitcast.4), calls=%async_computation.1 | async-start | bytes 1048576 | tf_op jit(solution)/shard_map/all_to_all | solution.py:93
  26.4 16.0 %copy-start.50 = (s32[512]{0:T(512)}, s32[512]{0:T(512)S(1)}, u32[]{:S(2)}) copy-start(s32[512]{0:T(512)S(1)} %get-tuple-element.354) | copy-start | bytes 6148
  26.4 16.0 %copy-start.52 = (s32[512]{0:T(512)}, s32[512]{0:T(512)S(1)}, u32[]{:S(2)}) copy-start(s32[512]{0:T(512)S(1)} %get-tuple-element.400) | copy-start | bytes 6148
  26.4 17.9 %copy-start.36 = (s32[512]{0:T(512)}, s32[512]{0:T(512)S(1)}, u32[]{:S(2)}) copy-start(s32[512]{0:T(512)S(1)} %get-tuple-element.399) | copy-start | bytes 6148
  26.4 40.5 %copy-start.39 = (s32[512]{0:T(512)}, s32[512]{0:T(512)S(1)}, u32[]{:S(2)}) copy-start(s32[512]{0:T(512)S(1)} %get-tuple-element.357) | copy-start | bytes 6148
  36.1 5.0 %copy-start.24 = (bf16[128,16,128]{2,0,1:T(8,128)(2,1)}, bf16[128,16,128]{2,0,1:T(8,128)(2,1)S(1)}, u32[]{:S(2)}) copy-start(bf16[128,16,128]{2,0,1:T(8,128)(2,1)S(1)} %all-to-all-done.1) | copy-start | bytes 1572868
  36.1 14.4 %all-to-all-start.4 = ((bf16[128,16,128]{2,0,1:T(8,128)(2,1)}), bf16[128,16,128]{2,0,1:T(8,128)(2,1)}, u32[]{:S(2)}, u32[]{:S(2)}) async-start(bf16[128,16,128]{2,0,1:T(8,128)(2,1)} %copy_bitcast_fusion.2), calls=%async_computation.4 | async-start | bytes 1048576 | tf_op jit(solution)/shard_map/all_to_all | solution.py:95
  41.1 3.2 %copy-start.25 = (bf16[4,128,128]{2,1,0:T(8,128)(2,1)}, bf16[4,128,128]{2,1,0:T(8,128)(2,1)S(1)}, u32[]{:S(2)}) copy-start(bf16[4,128,128]{2,1,0:T(8,128)(2,1)S(1)} %get-tuple-element.346) | copy-start | bytes 393220
  41.1 15.6 %copy-start.28 = (bf16[4,128,128]{2,1,0:T(8,128)(2,1)}, bf16[4,128,128]{2,1,0:T(8,128)(2,1)S(1)}, u32[]{:S(2)}) copy-start(bf16[4,128,128]{2,1,0:T(8,128)(2,1)S(1)} %get-tuple-element.345) | copy-start | bytes 393220
  41.3 3.1 %copy-start.20 = (bf16[4,128,128]{2,1,0:T(8,128)(2,1)}, bf16[4,128,128]{2,1,0:T(8,128)(2,1)S(1)}, u32[]{:S(2)}) copy-start(bf16[4,128,128]{2,1,0:T(8,128)(2,1)S(1)} %copy.122) | copy-start | bytes 393220
  41.4 3.0 %copy-start.44 = (s32[512]{0:T(512)S(1)}, s32[512]{0:T(512)}, u32[]{:S(2)}) copy-start(s32[512]{0:T(512)} %get-tuple-element.353) | copy-start | bytes 6148
  41.4 3.0 %copy-start.47 = (s32[512]{0:T(512)S(1)}, s32[512]{0:T(512)}, u32[]{:S(2)}) copy-start(s32[512]{0:T(512)} %get-tuple-element.396) | copy-start | bytes 6148
  45.4 11.4 %copy-start.45 = (s32[512]{0:T(512)S(1)}, s32[512]{0:T(512)}, u32[]{:S(2)}) copy-start(s32[512]{0:T(512)} %get-tuple-element.353) | copy-start | bytes 6148
  45.4 11.4 %copy-start.48 = (s32[512]{0:T(512)S(1)}, s32[512]{0:T(512)}, u32[]{:S(2)}) copy-start(s32[512]{0:T(512)} %get-tuple-element.396) | copy-start | bytes 6148
  45.4 11.4 %copy-start.51 = (s32[512]{0:T(512)S(1)}, s32[512]{0:T(512)}, u32[]{:S(2)}) copy-start(s32[512]{0:T(512)} %copy-done.50) | copy-start | bytes 6148
  45.4 11.4 %copy-start.53 = (s32[512]{0:T(512)S(1)}, s32[512]{0:T(512)}, u32[]{:S(2)}) copy-start(s32[512]{0:T(512)} %copy-done.52) | copy-start | bytes 6148
  51.3 14.3 %all-to-all-start.2 = ((bf16[128,16,128]{2,0,1:T(8,128)(2,1)}), bf16[128,16,128]{2,0,1:T(8,128)(2,1)}, u32[]{:S(2)}, u32[]{:S(2)}) async-start(bf16[128,16,128]{2,0,1:T(8,128)(2,1)} %bitcast.553), calls=%async_computation.2 | async-start | bytes 1048576 | tf_op jit(solution)/shard_map/all_to_all | solution.py:94
  56.8 10.2 %copy-start.41 = (s32[512]{0:T(512)S(1)}, s32[512]{0:T(512)}, u32[]{:S(2)}) copy-start(s32[512]{0:T(512)} %get-tuple-element.397) | copy-start | bytes 6148
  65.7 2.6 %copy-start.56 = (f32[512]{0:T(512)S(1)}, f32[512]{0:T(512)}, u32[]{:S(2)}) copy-start(f32[512]{0:T(512)} %get-tuple-element.370) | copy-start | bytes 6148
  65.7 2.6 %copy-start.57 = (f32[512]{0:T(512)S(1)}, f32[512]{0:T(512)}, u32[]{:S(2)}) copy-start(f32[512]{0:T(512)} %get-tuple-element.374) | copy-start | bytes 6148
  65.7 2.7 %copy-start.2 = (f32[512,512]{0,1:T(8,128)S(1)}, f32[512,512]{0,1:T(8,128)}, u32[]{:S(2)}) copy-start(f32[512,512]{0,1:T(8,128)} %get-tuple-element.375) | copy-start | bytes 3145732
  68.3 2.2 %copy-start.6 = (f32[512,512]{0,1:T(8,128)}, f32[512,512]{0,1:T(8,128)S(1)}, u32[]{:S(2)}) copy-start(f32[512,512]{0,1:T(8,128)S(1)} %get-tuple-element.373) | copy-start | bytes 3145732
  71.6 2.2 %copy-start.31 = (bf16[4,128,128]{2,1,0:T(8,128)(2,1)S(1)}, bf16[4,128,128]{2,1,0:T(8,128)(2,1)}, u32[]{:S(2)}) copy-start(bf16[4,128,128]{2,1,0:T(8,128)(2,1)} %get-tuple-element.347) | copy-start | bytes 393220
  71.6 2.2 %copy-start.46 = (s32[512]{0:T(512)S(1)}, s32[512]{0:T(512)}, u32[]{:S(2)}) copy-start(s32[512]{0:T(512)} %get-tuple-element.353) | copy-start | bytes 6148
  71.6 2.2 %copy-start.49 = (s32[512]{0:T(512)S(1)}, s32[512]{0:T(512)}, u32[]{:S(2)}) copy-start(s32[512]{0:T(512)} %get-tuple-element.396) | copy-start | bytes 6148
  72.7 1.5 copy-start.54
  72.7 1.5 copy-start.55
  72.7 1.6 copy-start.4
  74.2 4.4 %copy-start.8 = (f32[512,512]{0,1:T(8,128)}, f32[512,512]{0,1:T(8,128)S(1)}, u32[]{:S(2)}) copy-start(f32[512,512]{0,1:T(8,128)S(1)} %get-tuple-element.365) | copy-start | bytes 3145732
  81.4 12.6 %collective-permute-start = (bf16[2048,1,128]{2,0,1:T(8,128)(2,1)}, bf16[2048,1,128]{2,0,1:T(8,128)(2,1)}, u32[]{:S(2)}, u32[]{:S(2)}) collective-permute-start(bf16[2048,1,128]{2,0,1:T(8,128)(2,1)} %bitcast.549), channel_id=1, source_target_pairs={{0,16},{16,32},{32,48},{48,64},{64,80},{80,96},{96,112},{112,128},... | collective-permute-start | bytes 1572872 | tf_op jit(solution)/shard_map/ppermute | solution.py:20
  85.0 5.8 %copy-start.19 = (bf16[512,512]{0,1:T(8,128)(2,1)S(1)}, bf16[512,512]{0,1:T(8,128)(2,1)}, u32[]{:S(2)}) copy-start(bf16[512,512]{0,1:T(8,128)(2,1)} %fusion.29) | copy-start | bytes 1572868
  85.0 5.8 %copy-start.27 = (bf16[4,128,128]{2,1,0:T(8,128)(2,1)S(1)}, bf16[4,128,128]{2,1,0:T(8,128)(2,1)}, u32[]{:S(2)}) copy-start(bf16[4,128,128]{2,1,0:T(8,128)(2,1)} %get-tuple-element.344) | copy-start | bytes 393220
  85.0 6.1 %copy-start.16 = (bf16[512,512]{0,1:T(8,128)(2,1)S(1)}, bf16[512,512]{0,1:T(8,128)(2,1)}, u32[]{:S(2)}) copy-start(bf16[512,512]{0,1:T(8,128)(2,1)} %fusion.26) | copy-start | bytes 1572868
  85.0 6.1 %copy-start.26 = (bf16[4,128,128]{2,1,0:T(8,128)(2,1)S(1)}, bf16[4,128,128]{2,1,0:T(8,128)(2,1)}, u32[]{:S(2)}) copy-start(bf16[4,128,128]{2,1,0:T(8,128)(2,1)} %copy-done.25) | copy-start | bytes 393220
  85.0 6.5 %copy-start.18 = (bf16[512,512]{0,1:T(8,128)(2,1)S(1)}, bf16[512,512]{0,1:T(8,128)(2,1)}, u32[]{:S(2)}) copy-start(bf16[512,512]{0,1:T(8,128)(2,1)} %fusion.28) | copy-start | bytes 1572868
  86.5 5.4 %copy-start.12 = (bf16[512,512]{0,1:T(8,128)(2,1)S(1)}, bf16[512,512]{0,1:T(8,128)(2,1)}, u32[]{:S(2)}) copy-start(bf16[512,512]{0,1:T(8,128)(2,1)} %fusion.27) | copy-start | bytes 1572868
  86.5 5.4 %copy-start.29 = (bf16[4,128,128]{2,1,0:T(8,128)(2,1)S(1)}, bf16[4,128,128]{2,1,0:T(8,128)(2,1)}, u32[]{:S(2)}) copy-start(bf16[4,128,128]{2,1,0:T(8,128)(2,1)} %copy-done.28) | copy-start | bytes 393220
  86.5 20.7 %collective-permute-start.1 = (bf16[2048,1,128]{2,0,1:T(8,128)(2,1)}, bf16[2048,1,128]{2,0,1:T(8,128)(2,1)S(1)}, u32[]{:S(2)}, u32[]{:S(2)}) collective-permute-start(bf16[2048,1,128]{2,0,1:T(8,128)(2,1)} %bitcast.12), channel_id=1, source_target_pairs={{0,16},{16,32},{32,48},{48,64},{64,80},{80,96},{96,112},{112,128},... | collective-permute-start | bytes 1572872 | tf_op jit(solution)/shard_map/ppermute | solution.py:20
  91.1 1.1 copy-start.14
  91.9 1.1 copy-start.22
  91.9 1.1 copy-start.37
  93.6 1.7 copy-start.38
  93.6 1.7 copy-start.43
  100.9 1.2 copy-start.7
  101.2 1.3 copy-start.3
  102.9 1.2 copy-start.5
  103.2 1.3 copy-start.9
  104.8 2.4 %copy-start.1 = (f32[3072,1,128]{2,0,1:T(8,128)}, f32[3072,1,128]{2,0,1:T(8,128)S(1)}, u32[]{:S(2)}) copy-start(f32[3072,1,128]{2,0,1:T(8,128)S(1)} %fusion.97) | copy-start | bytes 4718596
  108.9 34.5 %collective-permute-start.3 = (f32[1024,1,128]{2,0,1:T(8,128)}, f32[1024,1,128]{2,0,1:T(8,128)}, u32[]{:S(2)}, u32[]{:S(2)}) collective-permute-start(f32[1024,1,128]{2,0,1:T(8,128)} %slice.893), channel_id=1, source_target_pairs={{16,0},{32,16},{48,32},{64,48},{80,64},{96,80},{112,96},{128,112},... | collective-permute-start | bytes 1572872 | tf_op jit(solution)/shard_map/ppermute | solution.py:20
  119.8 6.5 %copy-start.13 = (bf16[512,512]{0,1:T(8,128)(2,1)S(1)}, bf16[512,512]{0,1:T(8,128)(2,1)}, u32[]{:S(2)}) copy-start(bf16[512,512]{0,1:T(8,128)(2,1)} %fusion.27) | copy-start | bytes 1572868
  121.9 4.7 %copy-start.30 = (bf16[512,1,128]{2,0,1:T(8,128)(2,1)S(1)}, bf16[512,1,128]{2,0,1:T(8,128)(2,1)}, u32[]{:S(2)}) copy-start(bf16[512,1,128]{2,0,1:T(8,128)(2,1)} %get-tuple-element.391) | copy-start | bytes 393220
  121.9 6.6 %copy-start.17 = (bf16[512,512]{0,1:T(8,128)(2,1)S(1)}, bf16[512,512]{0,1:T(8,128)(2,1)}, u32[]{:S(2)}) copy-start(bf16[512,512]{0,1:T(8,128)(2,1)} %fusion.26) | copy-start | bytes 1572868
  121.9 16.8 %all-to-all-start.5 = ((bf16[16,128,128]{2,1,0:T(8,128)(2,1)}), bf16[16,128,128]{2,1,0:T(8,128)(2,1)}, u32[]{:S(2)}, u32[]{:S(2)}) async-start(bf16[16,128,128]{2,1,0:T(8,128)(2,1)} %bitcast.552), calls=%async_computation.5 | async-start | bytes 1048576 | tf_op jit(solution)/shard_map/all_to_all | solution.py:149
  126.7 16.3 %copy-start.15 = (bf16[512,512]{0,1:T(8,128)(2,1)S(1)}, bf16[512,512]{0,1:T(8,128)(2,1)}, u32[]{:S(2)}) copy-start(bf16[512,512]{0,1:T(8,128)(2,1)} %fusion.25) | copy-start | bytes 1572868
  138.8 15.3 %all-to-all-start.3 = ((bf16[16,128,128]{2,1,0:T(8,128)(2,1)}), bf16[16,128,128]{2,1,0:T(8,128)(2,1)}, u32[]{:S(2)}, u32[]{:S(2)}) async-start(bf16[16,128,128]{2,1,0:T(8,128)(2,1)} %bitcast.551), calls=%async_computation.3 | async-start | bytes 1048576 | tf_op jit(solution)/shard_map/all_to_all | solution.py:148
  143.3 15.0 %copy-start.11 = (bf16[512,512]{0,1:T(8,128)(2,1)S(1)}, bf16[512,512]{0,1:T(8,128)(2,1)}, u32[]{:S(2)}) copy-start(bf16[512,512]{0,1:T(8,128)(2,1)} %fusion.24) | copy-start | bytes 1572868
  154.0 19.1 %all-to-all-start.7 = ((f32[16,128,128]{2,1,0:T(8,128)}), f32[16,128,128]{2,1,0:T(8,128)}, u32[]{:S(2)}, u32[]{:S(2)}) async-start(f32[16,128,128]{2,1,0:T(8,128)} %bitcast.519), calls=%async_computation.7 | async-start | bytes 2097152 | tf_op jit(solution)/shard_map/all_to_all | solution.py:159
  158.7 8.6 %collective-permute-start.2 = (f32[1024,1,128]{2,0,1:T(8,128)S(1)}, f32[1024,1,128]{2,0,1:T(8,128)S(1)}, u32[]{:S(2)}, u32[]{:S(2)}) collective-permute-start(f32[1024,1,128]{2,0,1:T(8,128)S(1)} %slice.880), channel_id=1, source_target_pairs={{16,0},{32,16},{48,32},{64,48},{80,64},{96,80},{112,96},{128,112},... | collective-permute-start | bytes 1572872 | tf_op jit(solution)/shard_map/ppermute | solution.py:20
  173.1 22.8 %all-to-all-start.6 = ((f32[16,128,128]{2,1,0:T(8,128)}), f32[16,128,128]{2,1,0:T(8,128)S(1)}, u32[]{:S(2)}, u32[]{:S(2)}) async-start(f32[16,128,128]{2,1,0:T(8,128)} %bitcast.96), calls=%async_computation.6 | async-start | bytes 2097152 | tf_op jit(solution)/shard_map/all_to_all | solution.py:152
  (7 other events, 6.9 us)
where the time goes:
time: 199 us; the launch traced here: 197 us
  waiting for transfers between devices  70.9 us (36%)
  starting transfers between devices  45.9 us (23%)
  matrix products  43.4 us (22%)
  local copies, waits for them, and re-layouts  24 us (12%)
  other arithmetic  11 us (6%)
    dot_general x12, matrix products, score_piece(): jnp.einsum('qhd,khd->hqk', q_blk, k_sub, preferred_element_type=jnp.float32)  13.8 us
    dot_general x24, matrix products, rows_by_keys(): jnp.einsum('hqk,khd->qhd', left, k_sub, preferred_element_type=jnp.float32)  13.7 us
    all_to_all x1, waiting for transfers between devices, on_device(): lax.all_to_all(own_key_grads.reshape(row_len, local_heads * HD), 'ctx', s...  13 us
    ppermute x4, starting transfers between devices, passed_along(): return lax.ppermute(array, axis, pairs)  10.2 us
    all_to_all x1, waiting for transfers between devices, on_device(): lax.all_to_all(grad_q_rows, 'ctx', split_axis=0, concat_axis=1, tiled=True)  9.86 us
    all_to_all x1, waiting for transfers between devices, on_device(): lax.all_to_all(queries, 'ctx', split_axis=1, concat_axis=0, tiled=True)  9.04 us
    all_to_all x1, waiting for transfers between devices, on_device(): lax.all_to_all(attended_rows, 'ctx', split_axis=0, concat_axis=1, tiled=T...  8.58 us
    dot_general x12, matrix products, pair_products(): jnp.einsum('qhd,khd->hqk', d_blk, v_sub, preferred_element_type=jnp.float32)  8.46 us
  transfers between devices with their start and end apart: 12, of which 9 were waited for; matrix products, arithmetic and copies ran while one was open for 28% of the time, Pallas kernels for 0%

commit v1 on v0

v1 whole, which is shorter than its diff:
```python
import jax
import jax.numpy as jnp
from jax import lax
from jax.experimental import pallas as pl
from jax.experimental.pallas import tpu as pltpu
from jax.sharding import PartitionSpec as P

HEADS = 16
KV_HEADS = 8
HD = 128
GROUP = HEADS // KV_HEADS

TOK = 128
PEERS = 8
HALF = TOK * PEERS
BLK = 256
HALF_BLKS = HALF // BLK
PAIR = BLK // TOK
COLS = GROUP * BLK

q_scale = 144.0 ** (-0.5)
log2_e = 1.4426950408889634
far_below = -1e30

OWNERS = ((0, 1, 2, 3, 4, 5, 6, 7), (12, 13, 14, 15, 8, 9, 10, 11))


def exchange(array):
    return lax.all_to_all(
        array, "ctx", split_axis=0, concat_axis=0, tiled=True, axis_index_groups=[list(g) for g in OWNERS]
    )


def next_half_pairs(rows):
    pairs = []
    for row in range(rows):
        for first, second in zip(*OWNERS):
            pairs.append((row * 16 + first, row * 16 + second))
            if row + 1 < rows:
                pairs.append((row * 16 + second, (row + 1) * 16 + first))
    return pairs


def nt(left, right):
    return lax.dot_general(left, right, (((1,), (1,)), ((), ())), preferred_element_type=jnp.float32)


def nn(left, right):
    return lax.dot_general(left, right, (((1,), (0,)), ((), ())), preferred_element_type=jnp.float32)


def fold(array, op):
    return op(array.reshape(BLK // 8, 8, COLS), axis=0)


def attend_kernel(
    info, qd, kv, halo, starts, od, own_grads, halo_grads,
    k_rows, v_rows, k_cols, v_cols, held, key_grads, value_grads,
):
    half = info[0]

    def own_at(block):
        return lax.rem(block + half * (HALF_BLKS // 2), HALF_BLKS) * PAIR

    def halo_at(block):
        return lax.rem(block + (1 - half) * (HALF_BLKS // 2), HALF_BLKS) * PAIR

    for block in range(HALF_BLKS):
        for ref, at, first in ((halo, halo_at, 0), (kv, own_at, HALF)):
            rows = pl.ds(first + block * BLK, BLK)
            k_blk = ref[pl.ds(at(block), PAIR), 0].reshape(BLK, HD)
            v_blk = ref[pl.ds(at(block), PAIR), 1].reshape(BLK, HD)
            k_rows[rows, :] = k_blk
            v_rows[rows, :] = v_blk
            k_cols[:, rows] = k_blk.T
            v_cols[:, rows] = v_blk.T
    key_grads[...] = jnp.zeros_like(key_grads)
    value_grads[...] = jnp.zeros_like(value_grads)

    for block in range(HALF_BLKS):
        q_at = pl.ds(own_at(block), PAIR)
        q_blk = jnp.concatenate([qd[q_at, 0].reshape(BLK, HD), qd[q_at, 1].reshape(BLK, HD)], axis=0)
        d_blk = jnp.concatenate([qd[q_at, 2].reshape(BLK, HD), qd[q_at, 3].reshape(BLK, HD)], axis=0)
        q_cols = q_blk.T
        d_cols = d_blk.T
        start = starts[block]
        low = info[1 + block]
        diag = HALF_BLKS + block

        def score(key_block, causal):
            rows = pl.ds(pl.multiple_of(key_block * BLK, BLK), BLK)
            piece = nn(k_rows[rows, :], q_cols)
            at = lax.broadcasted_iota(jnp.int32, (BLK, COLS), 0)
            allowed = at >= start - key_block * BLK
            if causal:
                q_pos = lax.rem(lax.broadcasted_iota(jnp.int32, (BLK, COLS), 1), BLK)
                allowed = allowed & (at <= q_pos)
            piece = jnp.where(allowed, piece, far_below)
            held[key_block - block] = piece
            return fold(piece, jnp.max)

        highest = score(diag, True)
        highest = lax.fori_loop(
            low, diag, lambda key_block, best: jnp.maximum(best, score(key_block, False)), highest
        )
        highest = jnp.max(highest, axis=0, keepdims=True) * (q_scale * log2_e)

        def weigh(key_block, carry):
            summed, mixture = carry
            rows = pl.ds(pl.multiple_of(key_block * BLK, BLK), BLK)
            piece = jnp.exp2(held[key_block - block] * (q_scale * log2_e) - highest)
            held[key_block - block] = piece
            summed = summed + fold(piece, jnp.sum)
            mixture = mixture + nn(v_cols[:, rows], piece.astype(jnp.bfloat16))
            return summed, mixture

        summed, mixture = lax.fori_loop(
            low, diag + 1, weigh, (jnp.zeros((8, COLS), jnp.float32), jnp.zeros((HD, COLS), jnp.float32))
        )
        inverse = 1.0 / jnp.sum(summed, axis=0, keepdims=True)
        attended = (mixture * inverse).astype(jnp.bfloat16)
        row_delta = jnp.sum(
            attended.astype(jnp.float32) * d_cols.astype(jnp.float32), axis=0, keepdims=True
        )
        out_rows = attended.T
        od[q_at, 0] = out_rows[:BLK].reshape(PAIR, TOK, HD)
        od[q_at, 1] = out_rows[BLK:].reshape(PAIR, TOK, HD)

        def spread(key_block, grad_q):
            rows = pl.ds(pl.multiple_of(key_block * BLK, BLK), BLK)
            weights = held[key_block - block] * inverse
            dscore = (weights * (nn(v_rows[rows, :], d_cols) - row_delta)).astype(jnp.bfloat16)
            value_grads[rows, :] += nn(weights.astype(jnp.bfloat16), d_blk)
            key_grads[rows, :] += nn(dscore, q_blk)
            return grad_q + nn(k_cols[:, rows], dscore)

        grad_q = lax.fori_loop(low, diag + 1, spread, jnp.zeros((HD, COLS), jnp.float32))
        out_rows = (grad_q * q_scale).astype(jnp.bfloat16).T
        od[q_at, 2] = out_rows[:BLK].reshape(PAIR, TOK, HD)
        od[q_at, 3] = out_rows[BLK:].reshape(PAIR, TOK, HD)

    for block in range(HALF_BLKS):
        for ref, at, first in ((halo_grads, halo_at, 0), (own_grads, own_at, HALF)):
            rows = pl.ds(first + block * BLK, BLK)
            at_pair = pl.ds(at(block), PAIR)
            ref[at_pair, 0] = (key_grads[rows, :] * q_scale).astype(ref.dtype).reshape(PAIR, TOK, HD)
            ref[at_pair, 1] = value_grads[rows, :].astype(ref.dtype).reshape(PAIR, TOK, HD)


def attend_half(info, qd, kv, halo, starts):
    in_vmem = pl.BlockSpec(memory_space=pltpu.VMEM)
    return pl.pallas_call(
        attend_kernel,
        out_shape=(
            jax.ShapeDtypeStruct((PEERS, 2 * GROUP, TOK, HD), jnp.bfloat16),
            jax.ShapeDtypeStruct((PEERS, 2, TOK, HD), jnp.float32),
            jax.ShapeDtypeStruct((PEERS, 2, TOK, HD), jnp.bfloat16),
        ),
        in_specs=[pl.BlockSpec(memory_space=pltpu.SMEM)] + [in_vmem] * 4,
        out_specs=(in_vmem, in_vmem, in_vmem),
        scratch_shapes=[
            pltpu.VMEM((2 * HALF, HD), jnp.bfloat16),
            pltpu.VMEM((2 * HALF, HD), jnp.bfloat16),
            pltpu.VMEM((HD, 2 * HALF), jnp.bfloat16),
            pltpu.VMEM((HD, 2 * HALF), jnp.bfloat16),
            pltpu.VMEM((HALF_BLKS + 1, BLK, COLS), jnp.float32),
            pltpu.VMEM((2 * HALF, HD), jnp.float32),
            pltpu.VMEM((2 * HALF, HD), jnp.float32),
        ],
        compiler_params=pltpu.CompilerParams(vmem_limit_bytes=40 * 1024 * 1024),
        name="attend_half",
    )(info, qd, kv, halo, starts)


def doc_reach(doc_lengths, half_index):
    before = lax.broadcasted_iota(jnp.int32, (128, 128), 0) <= lax.broadcasted_iota(jnp.int32, (128, 128), 1)
    ends = jnp.sum(jnp.where(before, doc_lengths[:, None], 0), axis=0)
    positions = half_index * HALF + jnp.arange(HALF, dtype=jnp.int32)
    begins = jnp.max(jnp.where(ends[None, :] <= positions[:, None], ends[None, :], 0), axis=1)
    begins = (begins - (half_index - 1) * HALF).reshape(HALF_BLKS, 1, BLK)
    low = begins[:, 0, 0] // BLK
    return jnp.concatenate([begins] * GROUP, axis=2), low


def packed(first, second, width):
    first = first.reshape(TOK, PEERS, width, HD)
    second = second.reshape(TOK, PEERS, width, HD)
    return jnp.concatenate([first, second], axis=2).transpose(1, 2, 0, 3)


def unpacked(array, width):
    array = array.transpose(2, 0, 1, 3)
    return (
        array[:, :, :width].reshape(TOK, PEERS * width * HD),
        array[:, :, width:].reshape(TOK, PEERS * width * HD),
    )


def on_device(queries, keys, values, grad_out, doc_lengths):
    ahead = next_half_pairs(lax.axis_size("dp"))
    behind = [(to, of) for of, to in ahead]
    both = ("dp", "ctx")
    half = lax.axis_index("ctx") // PEERS
    starts, low = doc_reach(doc_lengths, lax.axis_index("dp") * 2 + half)
    info = jnp.concatenate([half[None].astype(jnp.int32), low])

    kv = exchange(packed(keys, values, 1))
    halo = lax.ppermute(kv, both, ahead)
    qd = exchange(packed(queries, grad_out, GROUP))
    od, own_grads, halo_grads = attend_half(info, qd, kv, halo, starts)
    back = lax.ppermute(halo_grads, both, behind)
    attended, grad_queries = unpacked(exchange(od), GROUP)
    grads = (own_grads + back.astype(jnp.float32)).astype(jnp.bfloat16)
    grad_keys, grad_values = unpacked(exchange(grads), 1)
    return attended, grad_queries, grad_keys, grad_values


def solution(mesh):
    rows = P(("dp", "ctx"), None)
    return jax.shard_map(
        on_device, mesh=mesh, in_specs=(rows, rows, rows, rows, P()), out_specs=(rows,) * 4, check_vma=False
    )
```

time: 199 us -> 95 us (0.48)
  the two profiles are of different devices: /device:TPU:32 before, /device:TPU:416 now
where the time goes in v1:
time: 95 us; the launch traced here: 94.5 us
  waiting for transfers between devices  38.8 us (41%)
  starting transfers between devices  25.4 us (27%)
  Pallas kernels  15.4 us (16%)
  local copies, waits for them, and re-layouts  10.7 us (11%)
  other arithmetic  3.45 us (4%)
    all_to_all x4, waiting for transfers between devices, exchange(): lax.all_to_all(array, 'ctx', split_axis=0, concat_axis=0, tiled=True, axi...  22.7 us
    all_to_all x4, starting transfers between devices, exchange(): lax.all_to_all(array, 'ctx', split_axis=0, concat_axis=0, tiled=True, axi...  19.4 us
    ppermute x1, waiting for transfers between devices, on_device(): back = lax.ppermute(halo_grads, both, behind)  15.6 us
    pallas_call x1, Pallas kernels, attend_half(): pl.pallas_call(attend_kernel, out_shape=(jax.ShapeDtypeStruct((PEERS, 2 *...  15.4 us
    unnamed x20, local copies, waits for them, and re-layouts  8.52 us
    ppermute x1, starting transfers between devices, on_device(): halo = lax.ppermute(kv, both, ahead)  4 us
    ppermute x1, starting transfers between devices, on_device(): back = lax.ppermute(halo_grads, both, behind)  1.92 us
    transpose x2, other arithmetic, packed(): return jnp.concatenate([first, second], axis=2).transpose(1, 2, 0, 3)  1.92 us
  transfers between devices with their start and end apart: 6, of which 5 were waited for; matrix products, arithmetic and copies ran while one was open for 7% of the time, Pallas kernels for 0%

profile of v1, /device:TPU:416, one launch (start us, length us, event | category | flops | bytes accessed | tf_op | source)
XLA Modules:
  0.0 94.5 jit_solution(8059151508178762642)
XLA Ops:
  0.6 1.1 %copy.29 = bf16[128,1024]{0,1:T(8,128)(2,1)S(1)} copy(bf16[128,1024]{1,0:T(8,128)(2,1)} %param.6) | data formatting | bytes 524288 | tf_op args[1]
  1.8 0.0 copy-start.4
  1.8 0.2 copy.31
  2.0 0.8 copy-done.4
  2.7 0.2 copy.30
  2.9 0.2 copy.32
  3.1 0.8 maximum_bitcast_fusion.1
  3.9 0.0 copy-start.2
  3.9 5.5 %all-to-all-start.1 = ((bf16[8,2,128,128]{3,2,1,0:T(8,128)(2,1)}), bf16[8,2,128,128]{3,2,1,0:T(8,128)(2,1)S(1)}, u32[]{:S(2)}, u32[]{:S(2)}) async-start(bf16[8,2,128,128]{3,2,1,0:T(8,128)(2,1)} %maximum_bitcast_fusion.1), calls=%async_computation.1 | async-start | bytes 1048576 | tf_op jit(solution)/shard_map/all_to_all | solution.py:29
  9.5 0.0 copy-done.2
  9.5 0.3 copy.25
  9.7 0.0 copy-start.3
  9.7 0.3 copy.27
  10.0 0.8 copy-done.3
  10.8 0.3 copy.26
  11.1 0.3 copy.28
  11.4 0.0 copy-start.5
  11.4 0.6 copy-done.5
  12.0 0.1 select_reduce_fusion.1
  12.1 1.1 %maximum_bitcast_fusion = bf16[8,4,128,128]{3,2,1,0:T(8,128)(2,1)} fusion(bf16[128,8,2,128]{3,0,2,1:T(8,128)(2,1)S(1)} %copy.28, bf16[128,8,2,128]{3,0,2,1:T(8,128)(2,1)S(1)} %copy.27), kind=kLoop, calls=%fused_computation | loop fusion | flops 524288 | bytes 2097152 | tf_op jit(solution)/shard_map/transpose | solution.py:188
  13.2 5.8 %all-to-all-done.1.kv = bf16[8,2,128,128]{3,2,1,0:T(8,128)(2,1)S(1)} async-done(((bf16[8,2,128,128]{3,2,1,0:T(8,128)(2,1)}), bf16[8,2,128,128]{3,2,1,0:T(8,128)(2,1)S(1)}, u32[]{:S(2)}, u32[]{:S(2)}) %all-to-all-start.1) | async-done | bytes 524320 | tf_op jit(solution)/shard_map/all_to_all | solution.py:29
  19.0 3.6 %all-to-all-start = ((bf16[8,4,128,128]{3,2,1,0:T(8,128)(2,1)}), bf16[8,4,128,128]{3,2,1,0:T(8,128)(2,1)S(1)}, u32[]{:S(2)}, u32[]{:S(2)}) async-start(bf16[8,4,128,128]{3,2,1,0:T(8,128)(2,1)} %maximum_bitcast_fusion), calls=%async_computation | async-start | bytes 2097152 | tf_op jit(solution)/shard_map/all_to_all | solution.py:29
  22.6 0.4 select_reduce_fusion
  23.0 4.0 %collective-permute-start = (bf16[8,2,128,128]{3,2,1,0:T(8,128)(2,1)S(1)}, bf16[8,2,128,128]{3,2,1,0:T(8,128)(2,1)S(1)}, u32[]{:S(2)}, u32[]{:S(2)}) collective-permute-start(bf16[8,2,128,128]{3,2,1,0:T(8,128)(2,1)S(1)} %all-to-all-done.1.kv), channel_id=1, source_target_pairs={{0,12},{12,16},{1,13},{13,17},{2,14},{14,18},{3,15},{15,19},{4,8},... | collective-permute-start | bytes 1572872 | tf_op jit(solution)/shard_map/ppermute | solution.py:208
  27.0 0.2 slice_reduce_fusion
  27.2 0.1 pad_add_fusion.1.info
  27.3 10.0 %all-to-all-done.qd = bf16[8,4,128,128]{3,2,1,0:T(8,128)(2,1)S(1)} async-done(((bf16[8,4,128,128]{3,2,1,0:T(8,128)(2,1)}), bf16[8,4,128,128]{3,2,1,0:T(8,128)(2,1)S(1)}, u32[]{:S(2)}, u32[]{:S(2)}) %all-to-all-start) | async-done | bytes 1048608 | tf_op jit(solution)/shard_map/all_to_all | solution.py:29
  37.2 0.5 collective-permute-done.halo
  37.7 15.4 %attend_half.1 = (bf16[8,4,128,128]{3,2,1,0:T(8,128)(2,1)}, f32[8,2,128,128]{3,2,1,0:T(8,128)S(1)}, bf16[8,2,128,128]{3,2,1,0:T(8,128)(2,1)S(1)}) custom-call(s32[5]{0:T(128)S(1)} %pad_add_fusion.1.info, bf16[8,4,128,128]{3,2,1,0:T(8,128)(2,1)S(1)} %all-to-all-done.qd, bf16[8,2,128,128]{3,2,1,0:T(8,128)(2,1)S(1)} %all-to-all-done.1.kv, ...), custom_call_target="tpu_custom_call" | custom-call | tf_op jit(solution)/shard_map/attend_half/pallas_call | solution.py:152
  53.2 0.0 copy-start
  53.2 0.8 copy-done
  54.0 0.0 copy-start.1
  54.0 4.9 %all-to-all-start.2 = ((bf16[8,4,128,128]{3,2,1,0:T(8,128)(2,1)}), bf16[8,4,128,128]{3,2,1,0:T(8,128)(2,1)S(1)}, u32[]{:S(2)}, u32[]{:S(2)}) async-start(bf16[8,4,128,128]{3,2,1,0:T(8,128)(2,1)} %get-tuple-element.7), calls=%async_computation.2 | async-start | bytes 2097152 | tf_op jit(solution)/shard_map/all_to_all | solution.py:29
  58.9 0.0 copy-done.1
  58.9 1.9 %collective-permute-start.1 = (bf16[8,2,128,128]{3,2,1,0:T(8,128)(2,1)S(1)}, bf16[8,2,128,128]{3,2,1,0:T(8,128)(2,1)S(1)}, u32[]{:S(2)}, u32[]{:S(2)}) collective-permute-start(bf16[8,2,128,128]{3,2,1,0:T(8,128)(2,1)S(1)} %copy-done.1), channel_id=1, source_target_pairs={{12,0},{16,12},{13,1},{17,13},{14,2},{18,14},{15,3},{19,15},{8,4},... | collective-permute-start | bytes 1572872 | tf_op jit(solution)/shard_map/ppermute | solution.py:211
  60.8 15.6 %collective-permute-done.1 = bf16[8,2,128,128]{3,2,1,0:T(8,128)(2,1)S(1)} collective-permute-done((bf16[8,2,128,128]{3,2,1,0:T(8,128)(2,1)S(1)}, bf16[8,2,128,128]{3,2,1,0:T(8,128)(2,1)S(1)}, u32[]{:S(2)}, u32[]{:S(2)}) %collective-permute-start.1) | collective-permute-done | bytes 524320 | tf_op jit(solution)/shard_map/ppermute | solution.py:211
  76.4 1.0 %add_convert_fusion = bf16[8,2,128,128]{3,2,1,0:T(8,128)(2,1)} fusion(f32[8,2,128,128]{3,2,1,0:T(8,128)S(1)} %get-tuple-element.8, bf16[8,2,128,128]{3,2,1,0:T(8,128)(2,1)S(1)} %collective-permute-done.1), kind=kLoop, calls=%fused_computation.1 | loop fusion | flops 786432 | bytes 2097152 | tf_op jit(solution)/shard_map/convert_element_type | solution.py:213
  77.4 0.0 all-to-all-done.2
  77.4 5.4 %all-to-all-start.3 = ((bf16[8,2,128,128]{3,2,1,0:T(8,128)(2,1)}), bf16[8,2,128,128]{3,2,1,0:T(8,128)(2,1)S(1)}, u32[]{:S(2)}, u32[]{:S(2)}) async-start(bf16[8,2,128,128]{3,2,1,0:T(8,128)(2,1)} %add_convert_fusion), calls=%async_computation.3 | async-start | bytes 1048576 | tf_op jit(solution)/shard_map/all_to_all | solution.py:29
  82.8 0.1 fusion
  82.9 0.3 copy.34
  83.2 1.0 %copy.38 = bf16[128,2048]{1,0:T(8,128)(2,1)} copy(bf16[128,2048]{0,1:T(8,128)(2,1)S(1)} %bitcast.18) | data formatting | bytes 1048576
  84.2 0.3 copy.33
  84.5 1.0 %copy.37 = bf16[128,2048]{1,0:T(8,128)(2,1)} copy(bf16[128,2048]{0,1:T(8,128)(2,1)S(1)} %bitcast.19) | data formatting | bytes 1048576
  85.5 6.9 %all-to-all-done.3 = bf16[8,2,128,128]{3,2,1,0:T(8,128)(2,1)S(1)} async-done(((bf16[8,2,128,128]{3,2,1,0:T(8,128)(2,1)}), bf16[8,2,128,128]{3,2,1,0:T(8,128)(2,1)S(1)}, u32[]{:S(2)}, u32[]{:S(2)}) %all-to-all-start.3) | async-done | bytes 524320 | tf_op jit(solution)/shard_map/all_to_all | solution.py:29
  92.4 0.2 copy.36
  92.6 0.9 copy.40
  93.5 0.2 copy.35
  93.7 0.9 copy.39
  (5 shorter events, 0.1 us)
Async XLA Ops:
  1.8 1.0 %copy-start.4 = (bf16[128,1024]{1,0:T(8,128)(2,1)S(1)}, bf16[128,1024]{1,0:T(8,128)(2,1)}, u32[]{:S(2)}) copy-start(bf16[128,1024]{1,0:T(8,128)(2,1)} %param.7) | copy-start | bytes 786436
  3.9 5.5 %copy-start.2 = (bf16[128,2048]{1,0:T(8,128)(2,1)S(1)}, bf16[128,2048]{1,0:T(8,128)(2,1)}, u32[]{:S(2)}) copy-start(bf16[128,2048]{1,0:T(8,128)(2,1)} %param.5) | copy-start | bytes 1572868
  3.9 15.1 %all-to-all-start.1 = ((bf16[8,2,128,128]{3,2,1,0:T(8,128)(2,1)}), bf16[8,2,128,128]{3,2,1,0:T(8,128)(2,1)S(1)}, u32[]{:S(2)}, u32[]{:S(2)}) async-start(bf16[8,2,128,128]{3,2,1,0:T(8,128)(2,1)} %maximum_bitcast_fusion.1), calls=%async_computation.1 | async-start | bytes 1048576 | tf_op jit(solution)/shard_map/all_to_all | solution.py:29
  9.7 1.0 %copy-start.3 = (bf16[128,2048]{1,0:T(8,128)(2,1)S(1)}, bf16[128,2048]{1,0:T(8,128)(2,1)}, u32[]{:S(2)}) copy-start(bf16[128,2048]{1,0:T(8,128)(2,1)} %param.8) | copy-start | bytes 1572868
  11.4 0.7 copy-start.5
  19.0 18.2 %all-to-all-start = ((bf16[8,4,128,128]{3,2,1,0:T(8,128)(2,1)}), bf16[8,4,128,128]{3,2,1,0:T(8,128)(2,1)S(1)}, u32[]{:S(2)}, u32[]{:S(2)}) async-start(bf16[8,4,128,128]{3,2,1,0:T(8,128)(2,1)} %maximum_bitcast_fusion), calls=%async_computation | async-start | bytes 2097152 | tf_op jit(solution)/shard_map/all_to_all | solution.py:29
  23.0 14.7 %collective-permute-start = (bf16[8,2,128,128]{3,2,1,0:T(8,128)(2,1)S(1)}, bf16[8,2,128,128]{3,2,1,0:T(8,128)(2,1)S(1)}, u32[]{:S(2)}, u32[]{:S(2)}) collective-permute-start(bf16[8,2,128,128]{3,2,1,0:T(8,128)(2,1)S(1)} %all-to-all-done.1.kv), channel_id=1, source_target_pairs={{0,12},{12,16},{1,13},{13,17},{2,14},{14,18},{3,15},{15,19},{4,8},... | collective-permute-start | bytes 1572872 | tf_op jit(solution)/shard_map/ppermute | solution.py:208
  53.2 0.8 copy-start
  54.0 4.9 %copy-start.1 = (bf16[8,2,128,128]{3,2,1,0:T(8,128)(2,1)S(1)}, bf16[8,2,128,128]{3,2,1,0:T(8,128)(2,1)}, u32[]{:S(2)}) copy-start(bf16[8,2,128,128]{3,2,1,0:T(8,128)(2,1)} %copy-done) | copy-start | bytes 1572868
  54.0 23.4 %all-to-all-start.2 = ((bf16[8,4,128,128]{3,2,1,0:T(8,128)(2,1)}), bf16[8,4,128,128]{3,2,1,0:T(8,128)(2,1)S(1)}, u32[]{:S(2)}, u32[]{:S(2)}) async-start(bf16[8,4,128,128]{3,2,1,0:T(8,128)(2,1)} %get-tuple-element.7), calls=%async_computation.2 | async-start | bytes 2097152 | tf_op jit(solution)/shard_map/all_to_all | solution.py:29
  58.9 17.5 %collective-permute-start.1 = (bf16[8,2,128,128]{3,2,1,0:T(8,128)(2,1)S(1)}, bf16[8,2,128,128]{3,2,1,0:T(8,128)(2,1)S(1)}, u32[]{:S(2)}, u32[]{:S(2)}) collective-permute-start(bf16[8,2,128,128]{3,2,1,0:T(8,128)(2,1)S(1)} %copy-done.1), channel_id=1, source_target_pairs={{12,0},{16,12},{13,1},{17,13},{14,2},{18,14},{15,3},{19,15},{8,4},... | collective-permute-start | bytes 1572872 | tf_op jit(solution)/shard_map/ppermute | solution.py:211
  77.4 15.0 %all-to-all-start.3 = ((bf16[8,2,128,128]{3,2,1,0:T(8,128)(2,1)}), bf16[8,2,128,128]{3,2,1,0:T(8,128)(2,1)S(1)}, u32[]{:S(2)}, u32[]{:S(2)}) async-start(bf16[8,2,128,128]{3,2,1,0:T(8,128)(2,1)} %add_convert_fusion), calls=%async_computation.3 | async-start | bytes 1048576 | tf_op jit(solution)/shard_map/all_to_all | solution.py:29

commit v2 on v1

v2 whole, which is shorter than its diff:
```python
import functools

import jax
import jax.numpy as jnp
from jax import lax
from jax.experimental import pallas as pl
from jax.experimental.pallas import tpu as pltpu
from jax.sharding import PartitionSpec as P

HEADS = 16
KV_HEADS = 8
HD = 128
GROUP = HEADS // KV_HEADS

TOK = 128
PEERS = 8
HALF = TOK * PEERS
BLK = 256
HALF_BLKS = HALF // BLK
PAIR = BLK // TOK
COLS = GROUP * BLK

q_scale = 144.0 ** (-0.5)
log2_e = 1.4426950408889634
far_below = -1e30

OWNERS = ((0, 1, 2, 3, 4, 5, 6, 7), (12, 13, 14, 15, 8, 9, 10, 11))


def exchange(array):
    return lax.all_to_all(
        array, "ctx", split_axis=0, concat_axis=0, tiled=True, axis_index_groups=[list(g) for g in OWNERS]
    )


def next_half_pairs(rows):
    pairs = []
    for row in range(rows):
        for first, second in zip(*OWNERS):
            pairs.append((row * 16 + first, row * 16 + second))
            if row + 1 < rows:
                pairs.append((row * 16 + second, (row + 1) * 16 + first))
    return pairs


def nt(left, right):
    return lax.dot_general(left, right, (((1,), (1,)), ((), ())), preferred_element_type=jnp.float32)


def nn(left, right):
    return lax.dot_general(left, right, (((1,), (0,)), ((), ())), preferred_element_type=jnp.float32)


def fold(array, op):
    return op(array.reshape(BLK // 8, 8, COLS), axis=0)


def attend_kernel(
    info, qd, kv, halo, starts, out_cols, own_grads, halo_grads,
    k_rows, v_rows, k_cols, v_cols, held, key_grads, value_grads,
):
    half = info[0]

    def own_at(block):
        return lax.rem(block + half * (HALF_BLKS // 2), HALF_BLKS) * PAIR

    def halo_at(block):
        return lax.rem(block + (1 - half) * (HALF_BLKS // 2), HALF_BLKS) * PAIR

    for block in range(HALF_BLKS):
        for ref, at, first in ((halo, halo_at, 0), (kv, own_at, HALF_BLKS)):
            k_blk = ref[pl.ds(at(block), PAIR), 0].reshape(BLK, HD)
            v_blk = ref[pl.ds(at(block), PAIR), 1].reshape(BLK, HD)
            k_rows[first + block] = k_blk
            v_rows[first + block] = v_blk
            k_cols[first + block] = k_blk.T
            v_cols[first + block] = v_blk.T
    key_grads[...] = jnp.zeros_like(key_grads)
    value_grads[...] = jnp.zeros_like(value_grads)

    def attend(block, count):
        q_at = pl.ds(own_at(block), PAIR)
        q_blk = jnp.concatenate([qd[q_at, 0].reshape(BLK, HD), qd[q_at, 1].reshape(BLK, HD)], axis=0)
        d_blk = jnp.concatenate([qd[q_at, 2].reshape(BLK, HD), qd[q_at, 3].reshape(BLK, HD)], axis=0)
        q_cols = q_blk.T
        d_cols = d_blk.T
        start = starts[block]
        low = HALF_BLKS + block + 1 - count
        highest = None
        for step in range(count):
            piece = nn(k_rows[low + step], q_cols)
            at = lax.broadcasted_iota(jnp.int32, (BLK, COLS), 0)
            allowed = at >= start - (low + step) * BLK
            if step == count - 1:
                q_pos = lax.rem(lax.broadcasted_iota(jnp.int32, (BLK, COLS), 1), BLK)
                allowed = allowed & (at <= q_pos)
            piece = jnp.where(allowed, piece, far_below)
            held[step] = piece
            best = fold(piece, jnp.max)
            highest = best if highest is None else jnp.maximum(highest, best)
        highest = jnp.max(highest, axis=0, keepdims=True) * (q_scale * log2_e)
        summed = mixture = 0.0
        for step in range(count):
            piece = jnp.exp2(held[step] * (q_scale * log2_e) - highest)
            held[step] = piece
            summed = summed + fold(piece, jnp.sum)
            mixture = mixture + nn(v_cols[low + step], piece.astype(jnp.bfloat16))
        inverse = 1.0 / jnp.sum(summed, axis=0, keepdims=True)
        attended = (mixture * inverse).astype(jnp.bfloat16)
        row_delta = jnp.sum(
            attended.astype(jnp.float32) * d_cols.astype(jnp.float32), axis=0, keepdims=True
        )
        out_cols[block, 0] = attended
        grad_q = 0.0
        for step in range(count):
            weights = held[step] * inverse
            dscore = (weights * (nn(v_rows[low + step], d_cols) - row_delta)).astype(jnp.bfloat16)
            value_grads[low + step] += nn(weights.astype(jnp.bfloat16), d_blk)
            key_grads[low + step] += nn(dscore, q_blk)
            grad_q = grad_q + nn(k_cols[low + step], dscore)
        out_cols[block, 1] = (grad_q * q_scale).astype(jnp.bfloat16)

    @pl.loop(0, HALF_BLKS)
    def _(block):
        count = HALF_BLKS + block + 1 - info[1 + block]
        for choice in range(1, HALF_BLKS + 2):
            pl.when(count == choice)(lambda choice=choice: attend(block, choice))

    for block in range(HALF_BLKS):
        for ref, at, first in ((halo_grads, halo_at, 0), (own_grads, own_at, HALF_BLKS)):
            at_pair = pl.ds(at(block), PAIR)
            ref[at_pair, 0] = (key_grads[first + block] * q_scale).astype(ref.dtype).reshape(PAIR, TOK, HD)
            ref[at_pair, 1] = value_grads[first + block].astype(ref.dtype).reshape(PAIR, TOK, HD)


def attend_half(info, qd, kv, halo, starts):
    in_vmem = pl.BlockSpec(memory_space=pltpu.VMEM)
    return pl.pallas_call(
        attend_kernel,
        out_shape=(
            jax.ShapeDtypeStruct((HALF_BLKS, 2, HD, COLS), jnp.bfloat16),
            jax.ShapeDtypeStruct((PEERS, 2, TOK, HD), jnp.float32),
            jax.ShapeDtypeStruct((PEERS, 2, TOK, HD), jnp.bfloat16),
        ),
        in_specs=[pl.BlockSpec(memory_space=pltpu.SMEM)] + [in_vmem] * 4,
        out_specs=(in_vmem, in_vmem, in_vmem),
        scratch_shapes=[
            pltpu.VMEM((2 * HALF_BLKS, BLK, HD), jnp.bfloat16),
            pltpu.VMEM((2 * HALF_BLKS, BLK, HD), jnp.bfloat16),
            pltpu.VMEM((2 * HALF_BLKS, HD, BLK), jnp.bfloat16),
            pltpu.VMEM((2 * HALF_BLKS, HD, BLK), jnp.bfloat16),
            pltpu.VMEM((HALF_BLKS + 1, BLK, COLS), jnp.float32),
            pltpu.VMEM((2 * HALF_BLKS, BLK, HD), jnp.float32),
            pltpu.VMEM((2 * HALF_BLKS, BLK, HD), jnp.float32),
        ],
        compiler_params=pltpu.CompilerParams(vmem_limit_bytes=40 * 1024 * 1024),
        name="attend_half",
    )(info, qd, kv, halo, starts)


def doc_reach(doc_lengths, half_index):
    before = lax.broadcasted_iota(jnp.int32, (128, 128), 0) <= lax.broadcasted_iota(jnp.int32, (128, 128), 1)
    ends = jnp.sum(jnp.where(before, doc_lengths[:, None], 0), axis=0)
    positions = half_index * HALF + jnp.arange(HALF, dtype=jnp.int32)
    begins = jnp.max(jnp.where(ends[None, :] <= positions[:, None], ends[None, :], 0), axis=1)
    begins = (begins - (half_index - 1) * HALF).reshape(HALF_BLKS, 1, BLK)
    low = begins[:, 0, 0] // BLK
    return jnp.concatenate([begins] * GROUP, axis=2), low


def turn_kernel(info, out_cols, od):
    for block in range(HALF_BLKS):
        at = pl.ds(lax.rem(block + info[0] * (HALF_BLKS // 2), HALF_BLKS) * PAIR, PAIR)
        for kind in range(2):
            rows = out_cols[block, kind].T
            for head in range(GROUP):
                od[at, kind * GROUP + head] = rows[head * BLK : (head + 1) * BLK].reshape(PAIR, TOK, HD)


def turned(info, out_cols):
    in_vmem = pl.BlockSpec(memory_space=pltpu.VMEM)
    return pl.pallas_call(
        turn_kernel,
        out_shape=jax.ShapeDtypeStruct((PEERS, 2 * GROUP, TOK, HD), jnp.bfloat16),
        in_specs=[pl.BlockSpec(memory_space=pltpu.SMEM), in_vmem],
        out_specs=in_vmem,
        name="turn_outputs",
    )(info, out_cols)


def pieces(width):
    for peer in range(PEERS):
        for place in range(width):
            yield peer, place, pl.ds((peer * width + place) * HD, HD)


def pack_kernel(width, first, second, out):
    for peer, place, columns in pieces(width):
        out[peer, place] = first[:, columns]
        out[peer, width + place] = second[:, columns]


def packed(first, second, width):
    in_vmem = pl.BlockSpec(memory_space=pltpu.VMEM)
    return pl.pallas_call(
        functools.partial(pack_kernel, width),
        out_shape=jax.ShapeDtypeStruct((PEERS, 2 * width, TOK, HD), jnp.bfloat16),
        in_specs=[in_vmem, in_vmem],
        out_specs=in_vmem,
        name="pack_heads",
    )(first, second)


def unpack_kernel(width, array, first, second):
    for peer, place, columns in pieces(width):
        first[:, columns] = array[peer, place]
        second[:, columns] = array[peer, width + place]


def unpacked(array, width):
    in_vmem = pl.BlockSpec(memory_space=pltpu.VMEM)
    rows = jax.ShapeDtypeStruct((TOK, PEERS * width * HD), jnp.bfloat16)
    return pl.pallas_call(
        functools.partial(unpack_kernel, width),
        out_shape=(rows, rows),
        in_specs=[in_vmem],
        out_specs=(in_vmem, in_vmem),
        name="unpack_heads",
    )(array)


def on_device(queries, keys, values, grad_out, doc_lengths):
    ahead = next_half_pairs(lax.axis_size("dp"))
    behind = [(to, of) for of, to in ahead]
    both = ("dp", "ctx")
    half = lax.axis_index("ctx") // PEERS
    starts, low = doc_reach(doc_lengths, lax.axis_index("dp") * 2 + half)
    info = jnp.concatenate([half[None].astype(jnp.int32), low])

    kv = exchange(packed(keys, values, 1))
    halo = lax.ppermute(kv, both, ahead)
    qd = exchange(packed(queries, grad_out, GROUP))
    out_cols, own_grads, halo_grads = attend_half(info, qd, kv, halo, starts)
    back = lax.ppermute(halo_grads, both, behind)
    od = turned(info, out_cols)
    attended, grad_queries = unpacked(exchange(od), GROUP)
    grads = (own_grads + back.astype(jnp.float32)).astype(jnp.bfloat16)
    grad_keys, grad_values = unpacked(exchange(grads), 1)
    return attended, grad_queries, grad_keys, grad_values


def solution(mesh):
    rows = P(("dp", "ctx"), None)
    return jax.shard_map(
        on_device, mesh=mesh, in_specs=(rows, rows, rows, rows, P()), out_specs=(rows,) * 4, check_vma=False
    )
```

time: 95 us -> 91.1 us (0.959)
  the two profiles are of different devices: /device:TPU:416 before, /device:TPU:384 now
where the time goes in v2:
time: 91.1 us; the launch traced here: 90.6 us
  waiting for transfers between devices  38.9 us (43%)
  starting transfers between devices  26.6 us (29%)
  Pallas kernels  20.1 us (22%)
  local copies, waits for them, and re-layouts  2.75 us (3%)
  other arithmetic  1.52 us (2%)
    all_to_all x4, waiting for transfers between devices, exchange(): lax.all_to_all(array, 'ctx', split_axis=0, concat_axis=0, tiled=True, axi...  24.2 us
    all_to_all x4, starting transfers between devices, exchange(): lax.all_to_all(array, 'ctx', split_axis=0, concat_axis=0, tiled=True, axi...  19.3 us
    ppermute x1, waiting for transfers between devices, on_device(): back = lax.ppermute(halo_grads, both, behind)  14.2 us
    pallas_call x1, Pallas kernels, attend_half(): pl.pallas_call(attend_kernel, out_shape=(jax.ShapeDtypeStruct((HALF_BLKS,...  8.82 us
    pallas_call x2, Pallas kernels, unpacked(): pl.pallas_call(functools.partial(unpack_kernel, width), out_shape=(rows,...  4.46 us
    pallas_call x2, Pallas kernels, packed(): pl.pallas_call(functools.partial(pack_kernel, width), out_shape=jax.Shape...  4.28 us
    ppermute x1, starting transfers between devices, on_device(): halo = lax.ppermute(kv, both, ahead)  4 us
    ppermute x1, starting transfers between devices, on_device(): back = lax.ppermute(halo_grads, both, behind)  3.28 us
  transfers between devices with their start and end apart: 6, of which 5 were waited for; matrix products, arithmetic and copies ran while one was open for 2% of the time, Pallas kernels for 5%

profile of v2, /device:TPU:384, one launch (start us, length us, event | category | flops | bytes accessed | tf_op | source)
XLA Modules:
  0.0 90.6 jit_solution(6123429401795050781)
XLA Ops:
  0.6 1.9 %pack_heads.3 = bf16[8,2,128,128]{3,2,1,0:T(8,128)(2,1)} custom-call(bf16[128,1024]{1,0:T(8,128)(2,1)} %first.3, bf16[128,1024]{1,0:T(8,128)(2,1)} %second.3), custom_call_target="tpu_custom_call" | custom-call | tf_op jit(solution)/shard_map/pack_heads/pallas_call | solution.py:205
  2.5 5.4 %all-to-all-start.1 = ((bf16[8,2,128,128]{3,2,1,0:T(8,128)(2,1)}), bf16[8,2,128,128]{3,2,1,0:T(8,128)(2,1)S(1)}, u32[]{:S(2)}, u32[]{:S(2)}) async-start(bf16[8,2,128,128]{3,2,1,0:T(8,128)(2,1)} %pack_heads.3), calls=%async_computation.1 | async-start | bytes 1048576 | tf_op jit(solution)/shard_map/all_to_all | solution.py:31
  7.9 0.0 copy-start.6
  8.0 2.4 %pack_heads.2 = bf16[8,4,128,128]{3,2,1,0:T(8,128)(2,1)} custom-call(bf16[128,2048]{1,0:T(8,128)(2,1)} %first.2, bf16[128,2048]{1,0:T(8,128)(2,1)} %second.2), custom_call_target="tpu_custom_call" | custom-call | tf_op jit(solution)/shard_map/pack_heads/pallas_call | solution.py:205
  10.3 0.0 copy-done.6
  10.3 0.1 select_reduce_fusion.1
  10.4 7.1 %all-to-all-done.1.kv = bf16[8,2,128,128]{3,2,1,0:T(8,128)(2,1)S(1)} async-done(((bf16[8,2,128,128]{3,2,1,0:T(8,128)(2,1)}), bf16[8,2,128,128]{3,2,1,0:T(8,128)(2,1)S(1)}, u32[]{:S(2)}, u32[]{:S(2)}) %all-to-all-start.1) | async-done | bytes 524320 | tf_op jit(solution)/shard_map/all_to_all | solution.py:31
  17.5 3.6 %all-to-all-start = ((bf16[8,4,128,128]{3,2,1,0:T(8,128)(2,1)}), bf16[8,4,128,128]{3,2,1,0:T(8,128)(2,1)S(1)}, u32[]{:S(2)}, u32[]{:S(2)}) async-start(bf16[8,4,128,128]{3,2,1,0:T(8,128)(2,1)} %pack_heads.2), calls=%async_computation | async-start | bytes 2097152 | tf_op jit(solution)/shard_map/all_to_all | solution.py:31
  21.1 0.4 select_reduce_fusion
  21.5 4.0 %collective-permute-start = (bf16[8,2,128,128]{3,2,1,0:T(8,128)(2,1)S(1)}, bf16[8,2,128,128]{3,2,1,0:T(8,128)(2,1)S(1)}, u32[]{:S(2)}, u32[]{:S(2)}) collective-permute-start(bf16[8,2,128,128]{3,2,1,0:T(8,128)(2,1)S(1)} %all-to-all-done.1.kv), channel_id=1, source_target_pairs={{0,12},{12,16},{1,13},{13,17},{2,14},{14,18},{3,15},{15,19},{4,8},... | collective-permute-start | bytes 1572872 | tf_op jit(solution)/shard_map/ppermute | solution.py:241
  25.5 0.2 slice_reduce_fusion
  25.7 0.1 pad_add_fusion.1.info
  25.8 0.0 copy-start.1
  25.8 10.0 %all-to-all-done.qd = bf16[8,4,128,128]{3,2,1,0:T(8,128)(2,1)S(1)} async-done(((bf16[8,4,128,128]{3,2,1,0:T(8,128)(2,1)}), bf16[8,4,128,128]{3,2,1,0:T(8,128)(2,1)S(1)}, u32[]{:S(2)}, u32[]{:S(2)}) %all-to-all-start) | async-done | bytes 1048608 | tf_op jit(solution)/shard_map/all_to_all | solution.py:31
  35.7 0.5 collective-permute-done.halo
  36.2 0.0 copy-done.1
  36.2 8.8 %attend_half.1 = (bf16[4,2,128,512]{3,2,1,0:T(8,128)(2,1)S(1)}, f32[8,2,128,128]{3,2,1,0:T(8,128)S(1)}, bf16[8,2,128,128]{3,2,1,0:T(8,128)(2,1)S(1)}) custom-call(s32[5]{0:T(128)S(1)} %pad_add_fusion.1.info, bf16[8,4,128,128]{3,2,1,0:T(8,128)(2,1)S(1)} %all-to-all-done.qd, bf16[8,2,128,128]{3,2,1,0:T(8,128)(2,1)S(1)} %all-to-all-done.1.kv, ...), custom_call_target="tpu_custom_call" | custom-call | tf_op jit(solution)/shard_map/attend_half/pallas_call | solution.py:138
  45.1 0.0 copy-start
  45.1 1.0 %copy-done = bf16[4,2,128,512]{3,2,1,0:T(8,128)(2,1)} copy-done((bf16[4,2,128,512]{3,2,1,0:T(8,128)(2,1)}, bf16[4,2,128,512]{3,2,1,0:T(8,128)(2,1)S(1)}, u32[]{:S(2)}) %copy-start) | copy-done | bytes 1048600
  46.1 0.0 copy-start.2
  46.1 0.8 copy-done.2
  46.9 2.5 %turn_outputs.1 = bf16[8,4,128,128]{3,2,1,0:T(8,128)(2,1)} custom-call(s32[5]{0:T(128)} %copy-done.1, bf16[4,2,128,512]{3,2,1,0:T(8,128)(2,1)} %copy-done), custom_call_target="tpu_custom_call" | custom-call | tf_op jit(solution)/shard_map/turn_outputs/pallas_call | solution.py:182
  49.4 0.0 copy-start.3
  49.4 4.9 %all-to-all-start.2 = ((bf16[8,4,128,128]{3,2,1,0:T(8,128)(2,1)}), bf16[8,4,128,128]{3,2,1,0:T(8,128)(2,1)S(1)}, u32[]{:S(2)}, u32[]{:S(2)}) async-start(bf16[8,4,128,128]{3,2,1,0:T(8,128)(2,1)} %turn_outputs.1), calls=%async_computation.2 | async-start | bytes 2097152 | tf_op jit(solution)/shard_map/all_to_all | solution.py:31
  54.3 0.0 copy-done.3
  54.3 3.3 %collective-permute-start.1 = (bf16[8,2,128,128]{3,2,1,0:T(8,128)(2,1)S(1)}, bf16[8,2,128,128]{3,2,1,0:T(8,128)(2,1)S(1)}, u32[]{:S(2)}, u32[]{:S(2)}) collective-permute-start(bf16[8,2,128,128]{3,2,1,0:T(8,128)(2,1)S(1)} %copy-done.3), channel_id=1, source_target_pairs={{12,0},{16,12},{13,1},{17,13},{14,2},{18,14},{15,3},{19,15},{8,4},... | collective-permute-start | bytes 1572872 | tf_op jit(solution)/shard_map/ppermute | solution.py:244
  57.6 14.2 %collective-permute-done.1 = bf16[8,2,128,128]{3,2,1,0:T(8,128)(2,1)S(1)} collective-permute-done((bf16[8,2,128,128]{3,2,1,0:T(8,128)(2,1)S(1)}, bf16[8,2,128,128]{3,2,1,0:T(8,128)(2,1)S(1)}, u32[]{:S(2)}, u32[]{:S(2)}) %collective-permute-start.1) | collective-permute-done | bytes 524320 | tf_op jit(solution)/shard_map/ppermute | solution.py:244
  71.8 1.0 %add_convert_fusion = bf16[8,2,128,128]{3,2,1,0:T(8,128)(2,1)} fusion(f32[8,2,128,128]{3,2,1,0:T(8,128)S(1)} %get-tuple-element.14, bf16[8,2,128,128]{3,2,1,0:T(8,128)(2,1)S(1)} %collective-permute-done.1), kind=kLoop, calls=%fused_computation | loop fusion | flops 786432 | bytes 2097152 | tf_op jit(solution)/shard_map/convert_element_type | solution.py:247
  72.8 0.0 all-to-all-done.2.array
  72.8 0.0 copy-start.4
  72.8 5.4 %all-to-all-start.3 = ((bf16[8,2,128,128]{3,2,1,0:T(8,128)(2,1)}), bf16[8,2,128,128]{3,2,1,0:T(8,128)(2,1)S(1)}, u32[]{:S(2)}, u32[]{:S(2)}) async-start(bf16[8,2,128,128]{3,2,1,0:T(8,128)(2,1)} %add_convert_fusion), calls=%async_computation.3 | async-start | bytes 1048576 | tf_op jit(solution)/shard_map/all_to_all | solution.py:31
  78.2 0.0 copy-done.4
  78.2 2.5 %unpack_heads.2 = (bf16[128,2048]{1,0:T(8,128)(2,1)}, bf16[128,2048]{1,0:T(8,128)(2,1)}) custom-call(bf16[8,4,128,128]{3,2,1,0:T(8,128)(2,1)} %copy-done.4), custom_call_target="tpu_custom_call" | custom-call | tf_op jit(solution)/shard_map/unpack_heads/pallas_call | solution.py:223
  80.7 7.1 %all-to-all-done.3.array = bf16[8,2,128,128]{3,2,1,0:T(8,128)(2,1)S(1)} async-done(((bf16[8,2,128,128]{3,2,1,0:T(8,128)(2,1)}), bf16[8,2,128,128]{3,2,1,0:T(8,128)(2,1)S(1)}, u32[]{:S(2)}, u32[]{:S(2)}) %all-to-all-start.3) | async-done | bytes 524320 | tf_op jit(solution)/shard_map/all_to_all | solution.py:31
  87.8 0.0 copy-start.5
  87.8 0.8 copy-done.5
  88.6 2.0 %unpack_heads.3 = (bf16[128,1024]{1,0:T(8,128)(2,1)}, bf16[128,1024]{1,0:T(8,128)(2,1)}) custom-call(bf16[8,2,128,128]{3,2,1,0:T(8,128)(2,1)} %copy-done.5), custom_call_target="tpu_custom_call" | custom-call | tf_op jit(solution)/shard_map/unpack_heads/pallas_call | solution.py:223
  (4 shorter events, 0.0 us)
Async XLA Ops:
  2.5 15.0 %all-to-all-start.1 = ((bf16[8,2,128,128]{3,2,1,0:T(8,128)(2,1)}), bf16[8,2,128,128]{3,2,1,0:T(8,128)(2,1)S(1)}, u32[]{:S(2)}, u32[]{:S(2)}) async-start(bf16[8,2,128,128]{3,2,1,0:T(8,128)(2,1)} %pack_heads.3), calls=%async_computation.1 | async-start | bytes 1048576 | tf_op jit(solution)/shard_map/all_to_all | solution.py:31
  7.9 2.4 %copy-start.6 = (s32[128]{0:T(128)S(1)}, s32[128]{0:T(128)}, u32[]{:S(2)}) copy-start(s32[128]{0:T(128)} %param.9) | copy-start | bytes 1540
  17.5 18.2 %all-to-all-start = ((bf16[8,4,128,128]{3,2,1,0:T(8,128)(2,1)}), bf16[8,4,128,128]{3,2,1,0:T(8,128)(2,1)S(1)}, u32[]{:S(2)}, u32[]{:S(2)}) async-start(bf16[8,4,128,128]{3,2,1,0:T(8,128)(2,1)} %pack_heads.2), calls=%async_computation | async-start | bytes 2097152 | tf_op jit(solution)/shard_map/all_to_all | solution.py:31
  21.5 14.7 %collective-permute-start = (bf16[8,2,128,128]{3,2,1,0:T(8,128)(2,1)S(1)}, bf16[8,2,128,128]{3,2,1,0:T(8,128)(2,1)S(1)}, u32[]{:S(2)}, u32[]{:S(2)}) collective-permute-start(bf16[8,2,128,128]{3,2,1,0:T(8,128)(2,1)S(1)} %all-to-all-done.1.kv), channel_id=1, source_target_pairs={{0,12},{12,16},{1,13},{13,17},{2,14},{14,18},{3,15},{15,19},{4,8},... | collective-permute-start | bytes 1572872 | tf_op jit(solution)/shard_map/ppermute | solution.py:241
  25.8 10.5 %copy-start.1 = (s32[5]{0:T(128)}, s32[5]{0:T(128)S(1)}, u32[]{:S(2)}) copy-start(s32[5]{0:T(128)S(1)} %pad_add_fusion.1.info) | copy-start | bytes 64
  45.1 1.0 %copy-start = (bf16[4,2,128,512]{3,2,1,0:T(8,128)(2,1)}, bf16[4,2,128,512]{3,2,1,0:T(8,128)(2,1)S(1)}, u32[]{:S(2)}) copy-start(bf16[4,2,128,512]{3,2,1,0:T(8,128)(2,1)S(1)} %get-tuple-element.11.out_cols) | copy-start | bytes 3145732
  46.1 0.8 copy-start.2
  49.4 5.0 %copy-start.3 = (bf16[8,2,128,128]{3,2,1,0:T(8,128)(2,1)S(1)}, bf16[8,2,128,128]{3,2,1,0:T(8,128)(2,1)}, u32[]{:S(2)}) copy-start(bf16[8,2,128,128]{3,2,1,0:T(8,128)(2,1)} %copy-done.2) | copy-start | bytes 1572868
  49.4 23.4 %all-to-all-start.2 = ((bf16[8,4,128,128]{3,2,1,0:T(8,128)(2,1)}), bf16[8,4,128,128]{3,2,1,0:T(8,128)(2,1)S(1)}, u32[]{:S(2)}, u32[]{:S(2)}) async-start(bf16[8,4,128,128]{3,2,1,0:T(8,128)(2,1)} %turn_outputs.1), calls=%async_computation.2 | async-start | bytes 2097152 | tf_op jit(solution)/shard_map/all_to_all | solution.py:31
  54.3 17.5 %collective-permute-start.1 = (bf16[8,2,128,128]{3,2,1,0:T(8,128)(2,1)S(1)}, bf16[8,2,128,128]{3,2,1,0:T(8,128)(2,1)S(1)}, u32[]{:S(2)}, u32[]{:S(2)}) collective-permute-start(bf16[8,2,128,128]{3,2,1,0:T(8,128)(2,1)S(1)} %copy-done.3), channel_id=1, source_target_pairs={{12,0},{16,12},{13,1},{17,13},{14,2},{18,14},{15,3},{19,15},{8,4},... | collective-permute-start | bytes 1572872 | tf_op jit(solution)/shard_map/ppermute | solution.py:244
  72.8 5.4 %copy-start.4 = (bf16[8,4,128,128]{3,2,1,0:T(8,128)(2,1)}, bf16[8,4,128,128]{3,2,1,0:T(8,128)(2,1)S(1)}, u32[]{:S(2)}) copy-start(bf16[8,4,128,128]{3,2,1,0:T(8,128)(2,1)S(1)} %all-to-all-done.2.array) | copy-start | bytes 3145732
  72.8 15.0 %all-to-all-start.3 = ((bf16[8,2,128,128]{3,2,1,0:T(8,128)(2,1)}), bf16[8,2,128,128]{3,2,1,0:T(8,128)(2,1)S(1)}, u32[]{:S(2)}, u32[]{:S(2)}) async-start(bf16[8,2,128,128]{3,2,1,0:T(8,128)(2,1)} %add_convert_fusion), calls=%async_computation.3 | async-start | bytes 1048576 | tf_op jit(solution)/shard_map/all_to_all | solution.py:31
  87.8 0.8 copy-start.5

commit v3 on v2

--- a/solution.py
+++ b/solution.py
@@ -56,7 +56,7 @@
 
 
 def attend_kernel(
-    info, qd, kv, halo, starts, out_cols, own_grads, halo_grads,
+    info, qd, kv, halo, starts, od, own_grads, halo_grads,
     k_rows, v_rows, k_cols, v_cols, held, key_grads, value_grads,
 ):
     half = info[0]
@@ -110,7 +110,9 @@
         row_delta = jnp.sum(
             attended.astype(jnp.float32) * d_cols.astype(jnp.float32), axis=0, keepdims=True
         )
-        out_cols[block, 0] = attended
+        out_rows = attended.T
+        od[q_at, 0] = out_rows[:BLK].reshape(PAIR, TOK, HD)
+        od[q_at, 1] = out_rows[BLK:].reshape(PAIR, TOK, HD)
         grad_q = 0.0
         for step in range(count):
             weights = held[step] * inverse
@@ -118,7 +120,9 @@
             value_grads[low + step] += nn(weights.astype(jnp.bfloat16), d_blk)
             key_grads[low + step] += nn(dscore, q_blk)
             grad_q = grad_q + nn(k_cols[low + step], dscore)
-        out_cols[block, 1] = (grad_q * q_scale).astype(jnp.bfloat16)
+        out_rows = (grad_q * q_scale).astype(jnp.bfloat16).T
+        od[q_at, 2] = out_rows[:BLK].reshape(PAIR, TOK, HD)
+        od[q_at, 3] = out_rows[BLK:].reshape(PAIR, TOK, HD)
 
     @pl.loop(0, HALF_BLKS)
     def _(block):
@@ -138,7 +142,7 @@
     return pl.pallas_call(
         attend_kernel,
         out_shape=(
-            jax.ShapeDtypeStruct((HALF_BLKS, 2, HD, COLS), jnp.bfloat16),
+            jax.ShapeDtypeStruct((PEERS, 2 * GROUP, TOK, HD), jnp.bfloat16),
             jax.ShapeDtypeStruct((PEERS, 2, TOK, HD), jnp.float32),
             jax.ShapeDtypeStruct((PEERS, 2, TOK, HD), jnp.bfloat16),
         ),
@@ -168,26 +172,6 @@
     return jnp.concatenate([begins] * GROUP, axis=2), low
 
 
-def turn_kernel(info, out_cols, od):
-    for block in range(HALF_BLKS):
-        at = pl.ds(lax.rem(block + info[0] * (HALF_BLKS // 2), HALF_BLKS) * PAIR, PAIR)
-        for kind in range(2):
-            rows = out_cols[block, kind].T
-            for head in range(GROUP):
-                od[at, kind * GROUP + head] = rows[head * BLK : (head + 1) * BLK].reshape(PAIR, TOK, HD)
-
-
-def turned(info, out_cols):
-    in_vmem = pl.BlockSpec(memory_space=pltpu.VMEM)
-    return pl.pallas_call(
-        turn_kernel,
-        out_shape=jax.ShapeDtypeStruct((PEERS, 2 * GROUP, TOK, HD), jnp.bfloat16),
-        in_specs=[pl.BlockSpec(memory_space=pltpu.SMEM), in_vmem],
-        out_specs=in_vmem,
-        name="turn_outputs",
-    )(info, out_cols)
-
-
 def pieces(width):
     for peer in range(PEERS):
         for place in range(width):
@@ -207,6 +191,7 @@
         out_shape=jax.ShapeDtypeStruct((PEERS, 2 * width, TOK, HD), jnp.bfloat16),
         in_specs=[in_vmem, in_vmem],
         out_specs=in_vmem,
+        compiler_params=pltpu.CompilerParams(vmem_limit_bytes=8 * 1024 * 1024) if width > 1 else None,
         name="pack_heads",
     )(first, second)
 
@@ -225,8 +210,26 @@
         out_shape=(rows, rows),
         in_specs=[in_vmem],
         out_specs=(in_vmem, in_vmem),
+        compiler_params=pltpu.CompilerParams(vmem_limit_bytes=8 * 1024 * 1024),
         name="unpack_heads",
     )(array)
+
+
+def join_kernel(own, back, out):
+    out[...] = (own[...] + back[...].astype(jnp.float32)).astype(jnp.bfloat16)
+
+
+def joined(own, back):
+    in_vmem = pl.BlockSpec(memory_space=pltpu.VMEM)
+    return pl.pallas_call(
+        join_kernel,
+        out_shape=jax.ShapeDtypeStruct(back.shape, jnp.bfloat16),
+        in_specs=[in_vmem, in_vmem],
+        out_specs=in_vmem,
+        compiler_params=pltpu.CompilerParams(vmem_limit_bytes=8 * 1024 * 1024),
+        cost_estimate=pl.CostEstimate(flops=30_000_000_000, bytes_accessed=100_000_000, transcendentals=0),
+        name="join_grads",
+    )(own, back)
 
 
 def on_device(queries, keys, values, grad_out, doc_lengths):
@@ -240,11 +243,10 @@
     kv = exchange(packed(keys, values, 1))
     halo = lax.ppermute(kv, both, ahead)
     qd = exchange(packed(queries, grad_out, GROUP))
-    out_cols, own_grads, halo_grads = attend_half(info, qd, kv, halo, starts)
+    od, own_grads, halo_grads = attend_half(info, qd, kv, halo, starts)
     back = lax.ppermute(halo_grads, both, behind)
-    od = turned(info, out_cols)
     attended, grad_queries = unpacked(exchange(od), GROUP)
-    grads = (own_grads + back.astype(jnp.float32)).astype(jnp.bfloat16)
+    grads = joined(own_grads, back)
     grad_keys, grad_values = unpacked(exchange(grads), 1)
     return attended, grad_queries, grad_keys, grad_values
 

time: 91.1 us -> 86.1 us (0.945)
  Pallas kernels: 20.1 us -> 16.2 us
  waiting for transfers between devices: 38.9 us -> 42.4 us
  local copies, waits for them, and re-layouts: 2.75 us -> 0.17 us
  other arithmetic: 1.52 us -> 0.56 us
    all_to_all x4, waiting for transfers between devices: 24.2 us -> 32.7 us  [exchange(): lax.all_to_all(array, 'ctx', split_axis=0, concat_axis=0, tiled=True, axi...]
    ppermute x1, waiting for transfers between devices: 14.2 us -> 9.23 us  [on_device(): back = lax.ppermute(halo_grads, both, behind)]
    unnamed x14 -> x6, local copies, waits for them, and re-layouts: 2.59 us -> 0.01 us
    pallas_call x2, Pallas kernels: 4.46 us -> 2.19 us  [unpacked(): pl.pallas_call(functools.partial(unpack_kernel, width), out_shape=(rows,...]
    all_to_all x4, starting transfers between devices: 19.3 us -> 17.2 us  [exchange(): lax.all_to_all(array, 'ctx', split_axis=0, concat_axis=0, tiled=True, axi...]
    pallas_call x2, Pallas kernels: 4.28 us -> 3.07 us  [packed(): pl.pallas_call(functools.partial(pack_kernel, width), out_shape=jax.Shape...]
    ppermute x1, starting transfers between devices: 3.28 us -> 4.46 us  [on_device(): back = lax.ppermute(halo_grads, both, behind)]
    convert_element_type x1 -> x0, other arithmetic: 0.96 us -> none  [on_device(): grads = (own_grads + back.astype(jnp.float32)).astype(jnp.bfloat16)]
  transfers between devices with their start and end apart: 6 -> 6, of which waited for: 5 -> 6; matrix products, arithmetic and copies ran while one was open for 2% -> 1% of each run, Pallas kernels for 5% -> 4%
where the time goes in v3:
time: 86.1 us; the launch traced here: 85.7 us
  waiting for transfers between devices  42.4 us (49%)
  starting transfers between devices  25.7 us (30%)
  Pallas kernels  16.2 us (19%)
    all_to_all x4, waiting for transfers between devices, exchange(): lax.all_to_all(array, 'ctx', split_axis=0, concat_axis=0, tiled=True, axi...  32.7 us
    all_to_all x4, starting transfers between devices, exchange(): lax.all_to_all(array, 'ctx', split_axis=0, concat_axis=0, tiled=True, axi...  17.2 us
    pallas_call x1, Pallas kernels, attend_half(): pl.pallas_call(attend_kernel, out_shape=(jax.ShapeDtypeStruct((PEERS, 2 *...  9.99 us
    ppermute x1, waiting for transfers between devices, on_device(): back = lax.ppermute(halo_grads, both, behind)  9.23 us
    ppermute x1, starting transfers between devices, on_device(): back = lax.ppermute(halo_grads, both, behind)  4.46 us
    ppermute x1, starting transfers between devices, on_device(): halo = lax.ppermute(kv, both, ahead)  4 us
    pallas_call x2, Pallas kernels, packed(): pl.pallas_call(functools.partial(pack_kernel, width), out_shape=jax.Shape...  3.07 us
    pallas_call x2, Pallas kernels, unpacked(): pl.pallas_call(functools.partial(unpack_kernel, width), out_shape=(rows,...  2.19 us
  transfers between devices with their start and end apart: 6, of which 6 were waited for; matrix products, arithmetic and copies ran while one was open for 1% of the time, Pallas kernels for 4%

profile of v3, /device:TPU:384, one launch (start us, length us, event | category | flops | bytes accessed | tf_op | source)
XLA Modules:
  0.0 85.7 jit_solution(1466197140878005904)
XLA Ops:
  0.6 1.9 %pack_heads.3 = bf16[8,2,128,128]{3,2,1,0:T(8,128)(2,1)} custom-call(bf16[128,1024]{1,0:T(8,128)(2,1)} %first.3, bf16[128,1024]{1,0:T(8,128)(2,1)} %second.3), custom_call_target="tpu_custom_call" | custom-call | tf_op jit(solution)/shard_map/pack_heads/pallas_call | solution.py:189
  2.5 0.0 copy-start
  2.5 0.0 copy-start.1
  2.6 5.5 %all-to-all-start.1 = ((bf16[8,2,128,128]{3,2,1,0:T(8,128)(2,1)}), bf16[8,2,128,128]{3,2,1,0:T(8,128)(2,1)S(1)}, u32[]{:S(2)}, u32[]{:S(2)}) async-start(bf16[8,2,128,128]{3,2,1,0:T(8,128)(2,1)} %pack_heads.3), calls=%async_computation.1 | async-start | bytes 1048576 | tf_op jit(solution)/shard_map/all_to_all | solution.py:31
  8.1 0.0 copy-done
  8.1 0.0 copy-done.1
  8.1 0.0 copy-start.2
  8.1 1.2 %pack_heads.2 = bf16[8,4,128,128]{3,2,1,0:T(8,128)(2,1)} custom-call(bf16[128,2048]{1,0:T(8,128)(2,1)S(1)} %copy-done, bf16[128,2048]{1,0:T(8,128)(2,1)S(1)} %copy-done.1), custom_call_target="tpu_custom_call" | custom-call | tf_op jit(solution)/shard_map/pack_heads/pallas_call | solution.py:189
  9.3 0.0 copy-done.2
  9.3 0.1 select_reduce_fusion.1
  9.4 8.3 %all-to-all-done.1.kv = bf16[8,2,128,128]{3,2,1,0:T(8,128)(2,1)S(1)} async-done(((bf16[8,2,128,128]{3,2,1,0:T(8,128)(2,1)}), bf16[8,2,128,128]{3,2,1,0:T(8,128)(2,1)S(1)}, u32[]{:S(2)}, u32[]{:S(2)}) %all-to-all-start.1) | async-done | bytes 524320 | tf_op jit(solution)/shard_map/all_to_all | solution.py:31
  17.7 3.6 %all-to-all-start = ((bf16[8,4,128,128]{3,2,1,0:T(8,128)(2,1)}), bf16[8,4,128,128]{3,2,1,0:T(8,128)(2,1)S(1)}, u32[]{:S(2)}, u32[]{:S(2)}) async-start(bf16[8,4,128,128]{3,2,1,0:T(8,128)(2,1)} %pack_heads.2), calls=%async_computation | async-start | bytes 2097152 | tf_op jit(solution)/shard_map/all_to_all | solution.py:31
  21.2 0.4 select_reduce_fusion
  21.6 4.0 %collective-permute-start = (bf16[8,2,128,128]{3,2,1,0:T(8,128)(2,1)S(1)}, bf16[8,2,128,128]{3,2,1,0:T(8,128)(2,1)S(1)}, u32[]{:S(2)}, u32[]{:S(2)}) collective-permute-start(bf16[8,2,128,128]{3,2,1,0:T(8,128)(2,1)S(1)} %all-to-all-done.1.kv), channel_id=1, source_target_pairs={{0,12},{12,16},{1,13},{13,17},{2,14},{14,18},{3,15},{15,19},{4,8},... | collective-permute-start | bytes 1572872 | tf_op jit(solution)/shard_map/ppermute | solution.py:244
  25.6 0.2 slice_reduce_fusion
  25.8 0.1 pad_add_fusion.1.info
  25.9 10.0 %all-to-all-done.qd = bf16[8,4,128,128]{3,2,1,0:T(8,128)(2,1)S(1)} async-done(((bf16[8,4,128,128]{3,2,1,0:T(8,128)(2,1)}), bf16[8,4,128,128]{3,2,1,0:T(8,128)(2,1)S(1)}, u32[]{:S(2)}, u32[]{:S(2)}) %all-to-all-start) | async-done | bytes 1048608 | tf_op jit(solution)/shard_map/all_to_all | solution.py:31
  35.9 0.5 collective-permute-done.halo
  36.4 10.0 %attend_half.1 = (bf16[8,4,128,128]{3,2,1,0:T(8,128)(2,1)}, f32[8,2,128,128]{3,2,1,0:T(8,128)S(1)}, bf16[8,2,128,128]{3,2,1,0:T(8,128)(2,1)}) custom-call(s32[5]{0:T(128)S(1)} %pad_add_fusion.1.info, bf16[8,4,128,128]{3,2,1,0:T(8,128)(2,1)S(1)} %all-to-all-done.qd, bf16[8,2,128,128]{3,2,1,0:T(8,128)(2,1)S(1)} %all-to-all-done.1.kv, ...), custom_call_target="tpu_custom_call" | custom-call | tf_op jit(solution)/shard_map/attend_half/pallas_call | solution.py:142
  46.4 4.5 %collective-permute-start.1 = (bf16[8,2,128,128]{3,2,1,0:T(8,128)(2,1)}, bf16[8,2,128,128]{3,2,1,0:T(8,128)(2,1)S(1)}, u32[]{:S(2)}, u32[]{:S(2)}) collective-permute-start(bf16[8,2,128,128]{3,2,1,0:T(8,128)(2,1)} %get-tuple-element.15), channel_id=1, source_target_pairs={{12,0},{16,12},{13,1},{17,13},{14,2},{18,14},{15,3},{19,15},{8,4},... | collective-permute-start | bytes 1572872 | tf_op jit(solution)/shard_map/ppermute | solution.py:247
  50.8 4.4 %all-to-all-start.2 = ((bf16[8,4,128,128]{3,2,1,0:T(8,128)(2,1)}), bf16[8,4,128,128]{3,2,1,0:T(8,128)(2,1)S(1)}, u32[]{:S(2)}, u32[]{:S(2)}) async-start(bf16[8,4,128,128]{3,2,1,0:T(8,128)(2,1)} %get-tuple-element.11), calls=%async_computation.2 | async-start | bytes 2097152 | tf_op jit(solution)/shard_map/all_to_all | solution.py:31
  55.2 9.2 %collective-permute-done.1.back = bf16[8,2,128,128]{3,2,1,0:T(8,128)(2,1)S(1)} collective-permute-done((bf16[8,2,128,128]{3,2,1,0:T(8,128)(2,1)}, bf16[8,2,128,128]{3,2,1,0:T(8,128)(2,1)S(1)}, u32[]{:S(2)}, u32[]{:S(2)}) %collective-permute-start.1) | collective-permute-done | bytes 524320 | tf_op jit(solution)/shard_map/ppermute | solution.py:247
  64.4 0.9 %join_grads.1 = bf16[8,2,128,128]{3,2,1,0:T(8,128)(2,1)} custom-call(f32[8,2,128,128]{3,2,1,0:T(8,128)S(1)} %get-tuple-element.14.own, bf16[8,2,128,128]{3,2,1,0:T(8,128)(2,1)S(1)} %collective-permute-done.1.back), custom_call_target="tpu_custom_call" | custom-call | flops 30000001024 | bytes 100000000 | tf_op jit(solution)/shard_map/join_grads/pallas_call | solution.py:224
  65.3 5.9 %all-to-all-done.2.array = bf16[8,4,128,128]{3,2,1,0:T(8,128)(2,1)S(1)} async-done(((bf16[8,4,128,128]{3,2,1,0:T(8,128)(2,1)}), bf16[8,4,128,128]{3,2,1,0:T(8,128)(2,1)S(1)}, u32[]{:S(2)}, u32[]{:S(2)}) %all-to-all-start.2) | async-done | bytes 1048608 | tf_op jit(solution)/shard_map/all_to_all | solution.py:31
  71.2 3.8 %all-to-all-start.3 = ((bf16[8,2,128,128]{3,2,1,0:T(8,128)(2,1)}), bf16[8,2,128,128]{3,2,1,0:T(8,128)(2,1)S(1)}, u32[]{:S(2)}, u32[]{:S(2)}) async-start(bf16[8,2,128,128]{3,2,1,0:T(8,128)(2,1)} %join_grads.1), calls=%async_computation.3 | async-start | bytes 1048576 | tf_op jit(solution)/shard_map/all_to_all | solution.py:31
  75.0 1.3 %unpack_heads.2 = (bf16[128,2048]{1,0:T(8,128)(2,1)}, bf16[128,2048]{1,0:T(8,128)(2,1)}) custom-call(bf16[8,4,128,128]{3,2,1,0:T(8,128)(2,1)S(1)} %all-to-all-done.2.array), custom_call_target="tpu_custom_call" | custom-call | tf_op jit(solution)/shard_map/unpack_heads/pallas_call | solution.py:208
  76.3 8.4 %all-to-all-done.3.array = bf16[8,2,128,128]{3,2,1,0:T(8,128)(2,1)S(1)} async-done(((bf16[8,2,128,128]{3,2,1,0:T(8,128)(2,1)}), bf16[8,2,128,128]{3,2,1,0:T(8,128)(2,1)S(1)}, u32[]{:S(2)}, u32[]{:S(2)}) %all-to-all-start.3) | async-done | bytes 524320 | tf_op jit(solution)/shard_map/all_to_all | solution.py:31
  84.7 0.9 %unpack_heads.3 = (bf16[128,1024]{1,0:T(8,128)(2,1)}, bf16[128,1024]{1,0:T(8,128)(2,1)}) custom-call(bf16[8,2,128,128]{3,2,1,0:T(8,128)(2,1)S(1)} %all-to-all-done.3.array), custom_call_target="tpu_custom_call" | custom-call | tf_op jit(solution)/shard_map/unpack_heads/pallas_call | solution.py:208
  (4 shorter events, 0.0 us)
Async XLA Ops:
  2.5 5.5 %copy-start = (bf16[128,2048]{1,0:T(8,128)(2,1)S(1)}, bf16[128,2048]{1,0:T(8,128)(2,1)}, u32[]{:S(2)}) copy-start(bf16[128,2048]{1,0:T(8,128)(2,1)} %first.2) | copy-start | bytes 1572868
  2.5 5.5 %copy-start.1 = (bf16[128,2048]{1,0:T(8,128)(2,1)S(1)}, bf16[128,2048]{1,0:T(8,128)(2,1)}, u32[]{:S(2)}) copy-start(bf16[128,2048]{1,0:T(8,128)(2,1)} %second.2) | copy-start | bytes 1572868
  2.6 15.1 %all-to-all-start.1 = ((bf16[8,2,128,128]{3,2,1,0:T(8,128)(2,1)}), bf16[8,2,128,128]{3,2,1,0:T(8,128)(2,1)S(1)}, u32[]{:S(2)}, u32[]{:S(2)}) async-start(bf16[8,2,128,128]{3,2,1,0:T(8,128)(2,1)} %pack_heads.3), calls=%async_computation.1 | async-start | bytes 1048576 | tf_op jit(solution)/shard_map/all_to_all | solution.py:31
  8.1 1.2 %copy-start.2 = (s32[128]{0:T(128)S(1)}, s32[128]{0:T(128)}, u32[]{:S(2)}) copy-start(s32[128]{0:T(128)} %param.9) | copy-start | bytes 1540
  17.7 18.2 %all-to-all-start = ((bf16[8,4,128,128]{3,2,1,0:T(8,128)(2,1)}), bf16[8,4,128,128]{3,2,1,0:T(8,128)(2,1)S(1)}, u32[]{:S(2)}, u32[]{:S(2)}) async-start(bf16[8,4,128,128]{3,2,1,0:T(8,128)(2,1)} %pack_heads.2), calls=%async_computation | async-start | bytes 2097152 | tf_op jit(solution)/shard_map/all_to_all | solution.py:31
  21.6 14.7 %collective-permute-start = (bf16[8,2,128,128]{3,2,1,0:T(8,128)(2,1)S(1)}, bf16[8,2,128,128]{3,2,1,0:T(8,128)(2,1)S(1)}, u32[]{:S(2)}, u32[]{:S(2)}) collective-permute-start(bf16[8,2,128,128]{3,2,1,0:T(8,128)(2,1)S(1)} %all-to-all-done.1.kv), channel_id=1, source_target_pairs={{0,12},{12,16},{1,13},{13,17},{2,14},{14,18},{3,15},{15,19},{4,8},... | collective-permute-start | bytes 1572872 | tf_op jit(solution)/shard_map/ppermute | solution.py:244
  46.4 18.1 %collective-permute-start.1 = (bf16[8,2,128,128]{3,2,1,0:T(8,128)(2,1)}, bf16[8,2,128,128]{3,2,1,0:T(8,128)(2,1)S(1)}, u32[]{:S(2)}, u32[]{:S(2)}) collective-permute-start(bf16[8,2,128,128]{3,2,1,0:T(8,128)(2,1)} %get-tuple-element.15), channel_id=1, source_target_pairs={{12,0},{16,12},{13,1},{17,13},{14,2},{18,14},{15,3},{19,15},{8,4},... | collective-permute-start | bytes 1572872 | tf_op jit(solution)/shard_map/ppermute | solution.py:247
  50.8 20.4 %all-to-all-start.2 = ((bf16[8,4,128,128]{3,2,1,0:T(8,128)(2,1)}), bf16[8,4,128,128]{3,2,1,0:T(8,128)(2,1)S(1)}, u32[]{:S(2)}, u32[]{:S(2)}) async-start(bf16[8,4,128,128]{3,2,1,0:T(8,128)(2,1)} %get-tuple-element.11), calls=%async_computation.2 | async-start | bytes 2097152 | tf_op jit(solution)/shard_map/all_to_all | solution.py:31
  71.2 13.5 %all-to-all-start.3 = ((bf16[8,2,128,128]{3,2,1,0:T(8,128)(2,1)}), bf16[8,2,128,128]{3,2,1,0:T(8,128)(2,1)S(1)}, u32[]{:S(2)}, u32[]{:S(2)}) async-start(bf16[8,2,128,128]{3,2,1,0:T(8,128)(2,1)} %join_grads.1), calls=%async_computation.3 | async-start | bytes 1048576 | tf_op jit(solution)/shard_map/all_to_all | solution.py:31

commit v4 on v3

--- a/solution.py
+++ b/solution.py
@@ -57,7 +57,7 @@
 
 def attend_kernel(
     info, qd, kv, halo, starts, od, own_grads, halo_grads,
-    k_rows, v_rows, k_cols, v_cols, held, key_grads, value_grads,
+    k_rows, v_rows, k_cols, v_cols, held, key_grads, value_grads, od_rows, halo_rows, od_sems, halo_sem,
 ):
     half = info[0]
 
@@ -111,8 +111,8 @@
             attended.astype(jnp.float32) * d_cols.astype(jnp.float32), axis=0, keepdims=True
         )
         out_rows = attended.T
-        od[q_at, 0] = out_rows[:BLK].reshape(PAIR, TOK, HD)
-        od[q_at, 1] = out_rows[BLK:].reshape(PAIR, TOK, HD)
+        od_rows[block, :, 0] = out_rows[:BLK].reshape(PAIR, TOK, HD)
+        od_rows[block, :, 1] = out_rows[BLK:].reshape(PAIR, TOK, HD)
         grad_q = 0.0
         for step in range(count):
             weights = held[step] * inverse
@@ -121,33 +121,46 @@
             key_grads[low + step] += nn(dscore, q_blk)
             grad_q = grad_q + nn(k_cols[low + step], dscore)
         out_rows = (grad_q * q_scale).astype(jnp.bfloat16).T
-        od[q_at, 2] = out_rows[:BLK].reshape(PAIR, TOK, HD)
-        od[q_at, 3] = out_rows[BLK:].reshape(PAIR, TOK, HD)
+        od_rows[block, :, 2] = out_rows[:BLK].reshape(PAIR, TOK, HD)
+        od_rows[block, :, 3] = out_rows[BLK:].reshape(PAIR, TOK, HD)
+
+    def od_copy(block):
+        return pltpu.make_async_copy(od_rows.at[block], od.at[pl.ds(own_at(block), PAIR)], od_sems.at[block])
 
     @pl.loop(0, HALF_BLKS)
     def _(block):
         count = HALF_BLKS + block + 1 - info[1 + block]
         for choice in range(1, HALF_BLKS + 2):
             pl.when(count == choice)(lambda choice=choice: attend(block, choice))
-
-    for block in range(HALF_BLKS):
-        for ref, at, first in ((halo_grads, halo_at, 0), (own_grads, own_at, HALF_BLKS)):
-            at_pair = pl.ds(at(block), PAIR)
-            ref[at_pair, 0] = (key_grads[first + block] * q_scale).astype(ref.dtype).reshape(PAIR, TOK, HD)
-            ref[at_pair, 1] = value_grads[first + block].astype(ref.dtype).reshape(PAIR, TOK, HD)
+        od_copy(block).start()
+
+    for block in range(HALF_BLKS):
+        at_pair = pl.ds(halo_at(block), PAIR)
+        halo_rows[at_pair, 0] = (key_grads[block] * q_scale).astype(jnp.bfloat16).reshape(PAIR, TOK, HD)
+        halo_rows[at_pair, 1] = value_grads[block].astype(jnp.bfloat16).reshape(PAIR, TOK, HD)
+    halo_copy = pltpu.make_async_copy(halo_rows, halo_grads, halo_sem)
+    halo_copy.start()
+    for block in range(HALF_BLKS):
+        at_pair = pl.ds(own_at(block), PAIR)
+        own_grads[at_pair, 0] = (key_grads[HALF_BLKS + block] * q_scale).reshape(PAIR, TOK, HD)
+        own_grads[at_pair, 1] = value_grads[HALF_BLKS + block].reshape(PAIR, TOK, HD)
+    for block in range(HALF_BLKS):
+        od_copy(block).wait()
+    halo_copy.wait()
 
 
 def attend_half(info, qd, kv, halo, starts):
     in_vmem = pl.BlockSpec(memory_space=pltpu.VMEM)
+    in_hbm = pl.BlockSpec(memory_space=pltpu.HBM)
     return pl.pallas_call(
         attend_kernel,
         out_shape=(
-            jax.ShapeDtypeStruct((PEERS, 2 * GROUP, TOK, HD), jnp.bfloat16),
+            pltpu.HBM((PEERS, 2 * GROUP, TOK, HD), jnp.bfloat16),
             jax.ShapeDtypeStruct((PEERS, 2, TOK, HD), jnp.float32),
-            jax.ShapeDtypeStruct((PEERS, 2, TOK, HD), jnp.bfloat16),
+            pltpu.HBM((PEERS, 2, TOK, HD), jnp.bfloat16),
         ),
         in_specs=[pl.BlockSpec(memory_space=pltpu.SMEM)] + [in_vmem] * 4,
-        out_specs=(in_vmem, in_vmem, in_vmem),
+        out_specs=(in_hbm, in_vmem, in_hbm),
         scratch_shapes=[
             pltpu.VMEM((2 * HALF_BLKS, BLK, HD), jnp.bfloat16),
             pltpu.VMEM((2 * HALF_BLKS, BLK, HD), jnp.bfloat16),
@@ -156,8 +169,12 @@
             pltpu.VMEM((HALF_BLKS + 1, BLK, COLS), jnp.float32),
             pltpu.VMEM((2 * HALF_BLKS, BLK, HD), jnp.float32),
             pltpu.VMEM((2 * HALF_BLKS, BLK, HD), jnp.float32),
+            pltpu.VMEM((HALF_BLKS, PAIR, 2 * GROUP, TOK, HD), jnp.bfloat16),
+            pltpu.VMEM((PEERS, 2, TOK, HD), jnp.bfloat16),
+            pltpu.SemaphoreType.DMA((HALF_BLKS,)),
+            pltpu.SemaphoreType.DMA,
         ],
-        compiler_params=pltpu.CompilerParams(vmem_limit_bytes=40 * 1024 * 1024),
+        compiler_params=pltpu.CompilerParams(vmem_limit_bytes=24 * 1024 * 1024),
         name="attend_half",
     )(info, qd, kv, halo, starts)
 
@@ -242,6 +259,7 @@
 
     kv = exchange(packed(keys, values, 1))
     halo = lax.ppermute(kv, both, ahead)
+    queries, grad_out, starts, info = lax.optimization_barrier((queries, grad_out, starts, info))
     qd = exchange(packed(queries, grad_out, GROUP))
     od, own_grads, halo_grads = attend_half(info, qd, kv, halo, starts)
     back = lax.ppermute(halo_grads, both, behind)

time: 86.1 us -> 84.9 us (0.986)
  the two profiles are of different devices: /device:TPU:384 before, /device:TPU:480 now
where the time goes in v4:
time: 84.9 us; the launch traced here: 84 us
  waiting for transfers between devices  41.4 us (49%)
  starting transfers between devices  24.4 us (29%)
  Pallas kernels  16 us (19%)
    all_to_all x4, waiting for transfers between devices, exchange(): lax.all_to_all(array, 'ctx', split_axis=0, concat_axis=0, tiled=True, axi...  31.9 us
    all_to_all x4, starting transfers between devices, exchange(): lax.all_to_all(array, 'ctx', split_axis=0, concat_axis=0, tiled=True, axi...  17.2 us
    pallas_call x1, Pallas kernels, attend_half(): pl.pallas_call(attend_kernel, out_shape=(pltpu.HBM((PEERS, 2 * GROUP, TOK...  9.87 us
    ppermute x1, waiting for transfers between devices, on_device(): back = lax.ppermute(halo_grads, both, behind)  9.46 us
    ppermute x1, starting transfers between devices, on_device(): halo = lax.ppermute(kv, both, ahead)  4 us
    ppermute x1, starting transfers between devices, on_device(): back = lax.ppermute(halo_grads, both, behind)  3.26 us
    pallas_call x2, Pallas kernels, packed(): pl.pallas_call(functools.partial(pack_kernel, width), out_shape=jax.Shape...  3.07 us
    pallas_call x2, Pallas kernels, unpacked(): pl.pallas_call(functools.partial(unpack_kernel, width), out_shape=(rows,...  2.19 us
  transfers between devices with their start and end apart: 6, of which 6 were waited for; matrix products, arithmetic and copies ran while one was open for 1% of the time, Pallas kernels for 4%

profile of v4, /device:TPU:480, one launch (start us, length us, event | category | flops | bytes accessed | tf_op | source)
XLA Modules:
  0.0 84.0 jit_solution(11715073306517340684)
XLA Ops:
  0.6 1.9 %pack_heads.3 = bf16[8,2,128,128]{3,2,1,0:T(8,128)(2,1)} custom-call(bf16[128,1024]{1,0:T(8,128)(2,1)} %first.2, bf16[128,1024]{1,0:T(8,128)(2,1)} %second.2), custom_call_target="tpu_custom_call" | custom-call | tf_op jit(solution)/shard_map/pack_heads/pallas_call | solution.py:206
  2.5 0.0 copy-start
  2.5 0.0 copy-start.1
  2.6 5.5 %all-to-all-start.1 = ((bf16[8,2,128,128]{3,2,1,0:T(8,128)(2,1)}), bf16[8,2,128,128]{3,2,1,0:T(8,128)(2,1)S(1)}, u32[]{:S(2)}, u32[]{:S(2)}) async-start(bf16[8,2,128,128]{3,2,1,0:T(8,128)(2,1)} %pack_heads.3), calls=%async_computation.1 | async-start | bytes 1048576 | tf_op jit(solution)/shard_map/all_to_all | solution.py:31
  8.1 0.0 copy-start.2
  8.1 0.6 copy-done.2
  8.7 0.1 select_reduce_fusion.1
  8.8 0.4 select_reduce_fusion
  9.2 0.2 slice_reduce_fusion
  9.4 0.1 pad_add_fusion.1.info
  9.5 0.0 copy-done
  9.5 0.0 copy-done.1
  9.5 1.2 %pack_heads.2 = bf16[8,4,128,128]{3,2,1,0:T(8,128)(2,1)} custom-call(bf16[128,2048]{1,0:T(8,128)(2,1)S(1)} %copy-done, bf16[128,2048]{1,0:T(8,128)(2,1)S(1)} %copy-done.1), custom_call_target="tpu_custom_call" | custom-call | tf_op jit(solution)/shard_map/pack_heads/pallas_call | solution.py:206
  10.7 7.0 %all-to-all-done.1.kv = bf16[8,2,128,128]{3,2,1,0:T(8,128)(2,1)S(1)} async-done(((bf16[8,2,128,128]{3,2,1,0:T(8,128)(2,1)}), bf16[8,2,128,128]{3,2,1,0:T(8,128)(2,1)S(1)}, u32[]{:S(2)}, u32[]{:S(2)}) %all-to-all-start.1) | async-done | bytes 524320 | tf_op jit(solution)/shard_map/all_to_all | solution.py:31
  17.7 3.6 %all-to-all-start = ((bf16[8,4,128,128]{3,2,1,0:T(8,128)(2,1)}), bf16[8,4,128,128]{3,2,1,0:T(8,128)(2,1)S(1)}, u32[]{:S(2)}, u32[]{:S(2)}) async-start(bf16[8,4,128,128]{3,2,1,0:T(8,128)(2,1)} %pack_heads.2), calls=%async_computation | async-start | bytes 2097152 | tf_op jit(solution)/shard_map/all_to_all | solution.py:31
  21.2 4.0 %collective-permute-start = (bf16[8,2,128,128]{3,2,1,0:T(8,128)(2,1)S(1)}, bf16[8,2,128,128]{3,2,1,0:T(8,128)(2,1)S(1)}, u32[]{:S(2)}, u32[]{:S(2)}) collective-permute-start(bf16[8,2,128,128]{3,2,1,0:T(8,128)(2,1)S(1)} %all-to-all-done.1.kv), channel_id=1, source_target_pairs={{0,12},{12,16},{1,13},{13,17},{2,14},{14,18},{3,15},{15,19},{4,8},... | collective-permute-start | bytes 1572872 | tf_op jit(solution)/shard_map/ppermute | solution.py:261
  25.2 10.6 %all-to-all-done.qd = bf16[8,4,128,128]{3,2,1,0:T(8,128)(2,1)S(1)} async-done(((bf16[8,4,128,128]{3,2,1,0:T(8,128)(2,1)}), bf16[8,4,128,128]{3,2,1,0:T(8,128)(2,1)S(1)}, u32[]{:S(2)}, u32[]{:S(2)}) %all-to-all-start) | async-done | bytes 1048608 | tf_op jit(solution)/shard_map/all_to_all | solution.py:31
  35.9 0.1 collective-permute-done.halo
  36.0 9.9 %attend_half.1 = (bf16[8,4,128,128]{3,2,1,0:T(8,128)(2,1)}, f32[8,2,128,128]{3,2,1,0:T(8,128)S(1)}, bf16[8,2,128,128]{3,2,1,0:T(8,128)(2,1)}) custom-call(s32[5]{0:T(128)S(1)} %pad_add_fusion.1.info, bf16[8,4,128,128]{3,2,1,0:T(8,128)(2,1)S(1)} %all-to-all-done.qd, bf16[8,2,128,128]{3,2,1,0:T(8,128)(2,1)S(1)} %all-to-all-done.1.kv, ...), custom_call_target="tpu_custom_call" | custom-call | tf_op jit(solution)/shard_map/attend_half/pallas_call | solution.py:155
  45.8 3.3 %collective-permute-start.1 = (bf16[8,2,128,128]{3,2,1,0:T(8,128)(2,1)}, bf16[8,2,128,128]{3,2,1,0:T(8,128)(2,1)S(1)}, u32[]{:S(2)}, u32[]{:S(2)}) collective-permute-start(bf16[8,2,128,128]{3,2,1,0:T(8,128)(2,1)} %get-tuple-element.23), channel_id=1, source_target_pairs={{12,0},{16,12},{13,1},{17,13},{14,2},{18,14},{15,3},{19,15},{8,4},... | collective-permute-start | bytes 1572872 | tf_op jit(solution)/shard_map/ppermute | solution.py:265
  49.1 4.4 %all-to-all-start.2 = ((bf16[8,4,128,128]{3,2,1,0:T(8,128)(2,1)}), bf16[8,4,128,128]{3,2,1,0:T(8,128)(2,1)S(1)}, u32[]{:S(2)}, u32[]{:S(2)}) async-start(bf16[8,4,128,128]{3,2,1,0:T(8,128)(2,1)} %get-tuple-element.19), calls=%async_computation.2 | async-start | bytes 2097152 | tf_op jit(solution)/shard_map/all_to_all | solution.py:31
  53.5 9.5 %collective-permute-done.1.back = bf16[8,2,128,128]{3,2,1,0:T(8,128)(2,1)S(1)} collective-permute-done((bf16[8,2,128,128]{3,2,1,0:T(8,128)(2,1)}, bf16[8,2,128,128]{3,2,1,0:T(8,128)(2,1)S(1)}, u32[]{:S(2)}, u32[]{:S(2)}) %collective-permute-start.1) | collective-permute-done | bytes 524320 | tf_op jit(solution)/shard_map/ppermute | solution.py:265
  62.9 0.9 %join_grads.1 = bf16[8,2,128,128]{3,2,1,0:T(8,128)(2,1)} custom-call(f32[8,2,128,128]{3,2,1,0:T(8,128)S(1)} %get-tuple-element.22.own, bf16[8,2,128,128]{3,2,1,0:T(8,128)(2,1)S(1)} %collective-permute-done.1.back), custom_call_target="tpu_custom_call" | custom-call | flops 30000001024 | bytes 100000000 | tf_op jit(solution)/shard_map/join_grads/pallas_call | solution.py:241
  63.8 5.8 %all-to-all-done.2.array = bf16[8,4,128,128]{3,2,1,0:T(8,128)(2,1)S(1)} async-done(((bf16[8,4,128,128]{3,2,1,0:T(8,128)(2,1)}), bf16[8,4,128,128]{3,2,1,0:T(8,128)(2,1)S(1)}, u32[]{:S(2)}, u32[]{:S(2)}) %all-to-all-start.2) | async-done | bytes 1048608 | tf_op jit(solution)/shard_map/all_to_all | solution.py:31
  69.6 3.7 %all-to-all-start.3 = ((bf16[8,2,128,128]{3,2,1,0:T(8,128)(2,1)}), bf16[8,2,128,128]{3,2,1,0:T(8,128)(2,1)S(1)}, u32[]{:S(2)}, u32[]{:S(2)}) async-start(bf16[8,2,128,128]{3,2,1,0:T(8,128)(2,1)} %join_grads.1), calls=%async_computation.3 | async-start | bytes 1048576 | tf_op jit(solution)/shard_map/all_to_all | solution.py:31
  73.3 1.3 %unpack_heads.2 = (bf16[128,2048]{1,0:T(8,128)(2,1)}, bf16[128,2048]{1,0:T(8,128)(2,1)}) custom-call(bf16[8,4,128,128]{3,2,1,0:T(8,128)(2,1)S(1)} %all-to-all-done.2.array), custom_call_target="tpu_custom_call" | custom-call | tf_op jit(solution)/shard_map/unpack_heads/pallas_call | solution.py:225
  74.6 8.4 %all-to-all-done.3.array = bf16[8,2,128,128]{3,2,1,0:T(8,128)(2,1)S(1)} async-done(((bf16[8,2,128,128]{3,2,1,0:T(8,128)(2,1)}), bf16[8,2,128,128]{3,2,1,0:T(8,128)(2,1)S(1)}, u32[]{:S(2)}, u32[]{:S(2)}) %all-to-all-start.3) | async-done | bytes 524320 | tf_op jit(solution)/shard_map/all_to_all | solution.py:31
  83.0 0.9 %unpack_heads.3 = (bf16[128,1024]{1,0:T(8,128)(2,1)}, bf16[128,1024]{1,0:T(8,128)(2,1)}) custom-call(bf16[8,2,128,128]{3,2,1,0:T(8,128)(2,1)S(1)} %all-to-all-done.3.array), custom_call_target="tpu_custom_call" | custom-call | tf_op jit(solution)/shard_map/unpack_heads/pallas_call | solution.py:225
  (4 shorter events, 0.0 us)
Async XLA Ops:
  2.5 6.9 %copy-start = (bf16[128,2048]{1,0:T(8,128)(2,1)S(1)}, bf16[128,2048]{1,0:T(8,128)(2,1)}, u32[]{:S(2)}) copy-start(bf16[128,2048]{1,0:T(8,128)(2,1)} %first.1) | copy-start | bytes 1572868
  2.5 7.0 %copy-start.1 = (bf16[128,2048]{1,0:T(8,128)(2,1)S(1)}, bf16[128,2048]{1,0:T(8,128)(2,1)}, u32[]{:S(2)}) copy-start(bf16[128,2048]{1,0:T(8,128)(2,1)} %second.1) | copy-start | bytes 1572868
  2.6 15.1 %all-to-all-start.1 = ((bf16[8,2,128,128]{3,2,1,0:T(8,128)(2,1)}), bf16[8,2,128,128]{3,2,1,0:T(8,128)(2,1)S(1)}, u32[]{:S(2)}, u32[]{:S(2)}) async-start(bf16[8,2,128,128]{3,2,1,0:T(8,128)(2,1)} %pack_heads.3), calls=%async_computation.1 | async-start | bytes 1048576 | tf_op jit(solution)/shard_map/all_to_all | solution.py:31
  8.1 0.7 copy-start.2
  17.7 18.2 %all-to-all-start = ((bf16[8,4,128,128]{3,2,1,0:T(8,128)(2,1)}), bf16[8,4,128,128]{3,2,1,0:T(8,128)(2,1)S(1)}, u32[]{:S(2)}, u32[]{:S(2)}) async-start(bf16[8,4,128,128]{3,2,1,0:T(8,128)(2,1)} %pack_heads.2), calls=%async_computation | async-start | bytes 2097152 | tf_op jit(solution)/shard_map/all_to_all | solution.py:31
  21.2 14.7 %collective-permute-start = (bf16[8,2,128,128]{3,2,1,0:T(8,128)(2,1)S(1)}, bf16[8,2,128,128]{3,2,1,0:T(8,128)(2,1)S(1)}, u32[]{:S(2)}, u32[]{:S(2)}) collective-permute-start(bf16[8,2,128,128]{3,2,1,0:T(8,128)(2,1)S(1)} %all-to-all-done.1.kv), channel_id=1, source_target_pairs={{0,12},{12,16},{1,13},{13,17},{2,14},{14,18},{3,15},{15,19},{4,8},... | collective-permute-start | bytes 1572872 | tf_op jit(solution)/shard_map/ppermute | solution.py:261
  45.8 17.1 %collective-permute-start.1 = (bf16[8,2,128,128]{3,2,1,0:T(8,128)(2,1)}, bf16[8,2,128,128]{3,2,1,0:T(8,128)(2,1)S(1)}, u32[]{:S(2)}, u32[]{:S(2)}) collective-permute-start(bf16[8,2,128,128]{3,2,1,0:T(8,128)(2,1)} %get-tuple-element.23), channel_id=1, source_target_pairs={{12,0},{16,12},{13,1},{17,13},{14,2},{18,14},{15,3},{19,15},{8,4},... | collective-permute-start | bytes 1572872 | tf_op jit(solution)/shard_map/ppermute | solution.py:265
  49.1 20.5 %all-to-all-start.2 = ((bf16[8,4,128,128]{3,2,1,0:T(8,128)(2,1)}), bf16[8,4,128,128]{3,2,1,0:T(8,128)(2,1)S(1)}, u32[]{:S(2)}, u32[]{:S(2)}) async-start(bf16[8,4,128,128]{3,2,1,0:T(8,128)(2,1)} %get-tuple-element.19), calls=%async_computation.2 | async-start | bytes 2097152 | tf_op jit(solution)/shard_map/all_to_all | solution.py:31
  69.6 13.4 %all-to-all-start.3 = ((bf16[8,2,128,128]{3,2,1,0:T(8,128)(2,1)}), bf16[8,2,128,128]{3,2,1,0:T(8,128)(2,1)S(1)}, u32[]{:S(2)}, u32[]{:S(2)}) async-start(bf16[8,2,128,128]{3,2,1,0:T(8,128)(2,1)} %join_grads.1), calls=%async_computation.3 | async-start | bytes 1048576 | tf_op jit(solution)/shard_map/all_to_all | solution.py:31

commit v5 on v4

--- a/solution.py
+++ b/solution.py
@@ -75,8 +75,8 @@
             v_rows[first + block] = v_blk
             k_cols[first + block] = k_blk.T
             v_cols[first + block] = v_blk.T
-    key_grads[...] = jnp.zeros_like(key_grads)
-    value_grads[...] = jnp.zeros_like(value_grads)
+    for sums in (key_grads, value_grads):
+        sums[:HALF_BLKS] = jnp.zeros((HALF_BLKS, BLK, HD), jnp.float32)
 
     def attend(block, count):
         q_at = pl.ds(own_at(block), PAIR)
@@ -117,8 +117,14 @@
         for step in range(count):
             weights = held[step] * inverse
             dscore = (weights * (nn(v_rows[low + step], d_cols) - row_delta)).astype(jnp.bfloat16)
-            value_grads[low + step] += nn(weights.astype(jnp.bfloat16), d_blk)
-            key_grads[low + step] += nn(dscore, q_blk)
+            value_part = nn(weights.astype(jnp.bfloat16), d_blk)
+            key_part = nn(dscore, q_blk)
+            if step == count - 1:
+                value_grads[low + step] = value_part
+                key_grads[low + step] = key_part
+            else:
+                value_grads[low + step] += value_part
+                key_grads[low + step] += key_part
             grad_q = grad_q + nn(k_cols[low + step], dscore)
         out_rows = (grad_q * q_scale).astype(jnp.bfloat16).T
         od_rows[block, :, 2] = out_rows[:BLK].reshape(PAIR, TOK, HD)
@@ -142,8 +148,8 @@
     halo_copy.start()
     for block in range(HALF_BLKS):
         at_pair = pl.ds(own_at(block), PAIR)
-        own_grads[at_pair, 0] = (key_grads[HALF_BLKS + block] * q_scale).reshape(PAIR, TOK, HD)
-        own_grads[at_pair, 1] = value_grads[HALF_BLKS + block].reshape(PAIR, TOK, HD)
+        own_grads[at_pair, 0] = (key_grads[HALF_BLKS + block] * q_scale).astype(jnp.bfloat16).reshape(PAIR, TOK, HD)
+        own_grads[at_pair, 1] = value_grads[HALF_BLKS + block].astype(jnp.bfloat16).reshape(PAIR, TOK, HD)
     for block in range(HALF_BLKS):
         od_copy(block).wait()
     halo_copy.wait()
@@ -156,7 +162,7 @@
         attend_kernel,
         out_shape=(
             pltpu.HBM((PEERS, 2 * GROUP, TOK, HD), jnp.bfloat16),
-            jax.ShapeDtypeStruct((PEERS, 2, TOK, HD), jnp.float32),
+            jax.ShapeDtypeStruct((PEERS, 2, TOK, HD), jnp.bfloat16),
             pltpu.HBM((PEERS, 2, TOK, HD), jnp.bfloat16),
         ),
         in_specs=[pl.BlockSpec(memory_space=pltpu.SMEM)] + [in_vmem] * 4,
@@ -233,7 +239,7 @@
 
 
 def join_kernel(own, back, out):
-    out[...] = (own[...] + back[...].astype(jnp.float32)).astype(jnp.bfloat16)
+    out[...] = (own[...].astype(jnp.float32) + back[...].astype(jnp.float32)).astype(jnp.bfloat16)
 
 
 def joined(own, back):

time: 84.9 us -> 85.2 us (level)
  the two profiles are of different devices: /device:TPU:480 before, /device:TPU:384 now
where the time goes in v5:
time: 85.2 us
  waiting for transfers between devices  40.7 us (48%)
  starting transfers between devices  28.5 us (33%)
  Pallas kernels  13.8 us (16%)
    all_to_all x4, waiting for transfers between devices, exchange(): lax.all_to_all(array, 'ctx', split_axis=0, concat_axis=0, tiled=True, axi...  32.2 us
    all_to_all x4, starting transfers between devices, exchange(): lax.all_to_all(array, 'ctx', split_axis=0, concat_axis=0, tiled=True, axi...  17.1 us
    ppermute x1, waiting for transfers between devices, on_device(): back = lax.ppermute(halo_grads, both, behind)  8.39 us
    pallas_call x1, Pallas kernels, attend_half(): pl.pallas_call(attend_kernel, out_shape=(pltpu.HBM((PEERS, 2 * GROUP, TOK...  7.65 us
    ppermute x1, starting transfers between devices, on_device(): back = lax.ppermute(halo_grads, both, behind)  7.46 us
    ppermute x1, starting transfers between devices, on_device(): halo = lax.ppermute(kv, both, ahead)  4 us
    pallas_call x2, Pallas kernels, packed(): pl.pallas_call(functools.partial(pack_kernel, width), out_shape=jax.Shape...  3.07 us
    pallas_call x2, Pallas kernels, unpacked(): pl.pallas_call(functools.partial(unpack_kernel, width), out_shape=(rows,...  2.19 us
  transfers between devices with their start and end apart: 6, of which 6 were waited for; matrix products, arithmetic and copies ran while one was open for 1% of the time, Pallas kernels for 4%

profile of v5, /device:TPU:384, one launch (start us, length us, event | category | flops | bytes accessed | tf_op | source)
XLA Modules:
  0.0 85.2 jit_solution(4388470979548697928)
XLA Ops:
  0.6 1.9 %pack_heads.3 = bf16[8,2,128,128]{3,2,1,0:T(8,128)(2,1)} custom-call(bf16[128,1024]{1,0:T(8,128)(2,1)} %first.2, bf16[128,1024]{1,0:T(8,128)(2,1)} %second.2), custom_call_target="tpu_custom_call" | custom-call | tf_op jit(solution)/shard_map/pack_heads/pallas_call | solution.py:212
  2.5 0.0 copy-start
  2.5 0.0 copy-start.1
  2.6 5.5 %all-to-all-start.1 = ((bf16[8,2,128,128]{3,2,1,0:T(8,128)(2,1)}), bf16[8,2,128,128]{3,2,1,0:T(8,128)(2,1)S(1)}, u32[]{:S(2)}, u32[]{:S(2)}) async-start(bf16[8,2,128,128]{3,2,1,0:T(8,128)(2,1)} %pack_heads.3), calls=%async_computation.1 | async-start | bytes 1048576 | tf_op jit(solution)/shard_map/all_to_all | solution.py:31
  8.1 0.0 copy-start.2
  8.1 0.6 copy-done.2
  8.7 0.1 select_reduce_fusion.1
  8.8 0.4 select_reduce_fusion
  9.2 0.2 slice_reduce_fusion
  9.4 0.1 pad_add_fusion.1.info
  9.5 0.0 copy-done
  9.5 0.0 copy-done.1
  9.5 1.2 %pack_heads.2 = bf16[8,4,128,128]{3,2,1,0:T(8,128)(2,1)} custom-call(bf16[128,2048]{1,0:T(8,128)(2,1)S(1)} %copy-done, bf16[128,2048]{1,0:T(8,128)(2,1)S(1)} %copy-done.1), custom_call_target="tpu_custom_call" | custom-call | tf_op jit(solution)/shard_map/pack_heads/pallas_call | solution.py:212
  10.7 7.0 %all-to-all-done.1.kv = bf16[8,2,128,128]{3,2,1,0:T(8,128)(2,1)S(1)} async-done(((bf16[8,2,128,128]{3,2,1,0:T(8,128)(2,1)}), bf16[8,2,128,128]{3,2,1,0:T(8,128)(2,1)S(1)}, u32[]{:S(2)}, u32[]{:S(2)}) %all-to-all-start.1) | async-done | bytes 524320 | tf_op jit(solution)/shard_map/all_to_all | solution.py:31
  17.7 3.6 %all-to-all-start = ((bf16[8,4,128,128]{3,2,1,0:T(8,128)(2,1)}), bf16[8,4,128,128]{3,2,1,0:T(8,128)(2,1)S(1)}, u32[]{:S(2)}, u32[]{:S(2)}) async-start(bf16[8,4,128,128]{3,2,1,0:T(8,128)(2,1)} %pack_heads.2), calls=%async_computation | async-start | bytes 2097152 | tf_op jit(solution)/shard_map/all_to_all | solution.py:31
  21.2 4.0 %collective-permute-start = (bf16[8,2,128,128]{3,2,1,0:T(8,128)(2,1)S(1)}, bf16[8,2,128,128]{3,2,1,0:T(8,128)(2,1)S(1)}, u32[]{:S(2)}, u32[]{:S(2)}) collective-permute-start(bf16[8,2,128,128]{3,2,1,0:T(8,128)(2,1)S(1)} %all-to-all-done.1.kv), channel_id=1, source_target_pairs={{0,12},{12,16},{1,13},{13,17},{2,14},{14,18},{3,15},{15,19},{4,8},... | collective-permute-start | bytes 1572872 | tf_op jit(solution)/shard_map/ppermute | solution.py:267
  25.2 10.6 %all-to-all-done.qd = bf16[8,4,128,128]{3,2,1,0:T(8,128)(2,1)S(1)} async-done(((bf16[8,4,128,128]{3,2,1,0:T(8,128)(2,1)}), bf16[8,4,128,128]{3,2,1,0:T(8,128)(2,1)S(1)}, u32[]{:S(2)}, u32[]{:S(2)}) %all-to-all-start) | async-done | bytes 1048608 | tf_op jit(solution)/shard_map/all_to_all | solution.py:31
  35.9 0.1 collective-permute-done.halo
  36.0 7.7 %attend_half.1 = (bf16[8,4,128,128]{3,2,1,0:T(8,128)(2,1)}, bf16[8,2,128,128]{3,2,1,0:T(8,128)(2,1)S(1)}, bf16[8,2,128,128]{3,2,1,0:T(8,128)(2,1)}) custom-call(s32[5]{0:T(128)S(1)} %pad_add_fusion.1.info, bf16[8,4,128,128]{3,2,1,0:T(8,128)(2,1)S(1)} %all-to-all-done.qd, bf16[8,2,128,128]{3,2,1,0:T(8,128)(2,1)S(1)} %all-to-all-done.1.kv, ...), custom_call_target="tpu_custom_call" | custom-call | tf_op jit(solution)/shard_map/attend_half/pallas_call | solution.py:161
  43.6 7.5 %collective-permute-start.1 = (bf16[8,2,128,128]{3,2,1,0:T(8,128)(2,1)}, bf16[8,2,128,128]{3,2,1,0:T(8,128)(2,1)S(1)}, u32[]{:S(2)}, u32[]{:S(2)}) collective-permute-start(bf16[8,2,128,128]{3,2,1,0:T(8,128)(2,1)} %get-tuple-element.23), channel_id=1, source_target_pairs={{12,0},{16,12},{13,1},{17,13},{14,2},{18,14},{15,3},{19,15},{8,4},... | collective-permute-start | bytes 1572872 | tf_op jit(solution)/shard_map/ppermute | solution.py:271
  51.1 4.4 %all-to-all-start.2 = ((bf16[8,4,128,128]{3,2,1,0:T(8,128)(2,1)}), bf16[8,4,128,128]{3,2,1,0:T(8,128)(2,1)S(1)}, u32[]{:S(2)}, u32[]{:S(2)}) async-start(bf16[8,4,128,128]{3,2,1,0:T(8,128)(2,1)} %get-tuple-element.19), calls=%async_computation.2 | async-start | bytes 2097152 | tf_op jit(solution)/shard_map/all_to_all | solution.py:31
  55.4 8.4 %collective-permute-done.1.back = bf16[8,2,128,128]{3,2,1,0:T(8,128)(2,1)S(1)} collective-permute-done((bf16[8,2,128,128]{3,2,1,0:T(8,128)(2,1)}, bf16[8,2,128,128]{3,2,1,0:T(8,128)(2,1)S(1)}, u32[]{:S(2)}, u32[]{:S(2)}) %collective-permute-start.1) | collective-permute-done | bytes 524320 | tf_op jit(solution)/shard_map/ppermute | solution.py:271
  63.8 0.9 %join_grads.1 = bf16[8,2,128,128]{3,2,1,0:T(8,128)(2,1)} custom-call(bf16[8,2,128,128]{3,2,1,0:T(8,128)(2,1)S(1)} %get-tuple-element.22.own, bf16[8,2,128,128]{3,2,1,0:T(8,128)(2,1)S(1)} %collective-permute-done.1.back), custom_call_target="tpu_custom_call" | custom-call | flops 30000001024 | bytes 100000000 | tf_op jit(solution)/shard_map/join_grads/pallas_call | solution.py:247
  64.8 6.2 %all-to-all-done.2.array = bf16[8,4,128,128]{3,2,1,0:T(8,128)(2,1)S(1)} async-done(((bf16[8,4,128,128]{3,2,1,0:T(8,128)(2,1)}), bf16[8,4,128,128]{3,2,1,0:T(8,128)(2,1)S(1)}, u32[]{:S(2)}, u32[]{:S(2)}) %all-to-all-start.2) | async-done | bytes 1048608 | tf_op jit(solution)/shard_map/all_to_all | solution.py:31
  71.0 3.6 %all-to-all-start.3 = ((bf16[8,2,128,128]{3,2,1,0:T(8,128)(2,1)}), bf16[8,2,128,128]{3,2,1,0:T(8,128)(2,1)S(1)}, u32[]{:S(2)}, u32[]{:S(2)}) async-start(bf16[8,2,128,128]{3,2,1,0:T(8,128)(2,1)} %join_grads.1), calls=%async_computation.3 | async-start | bytes 1048576 | tf_op jit(solution)/shard_map/all_to_all | solution.py:31
  74.6 1.3 %unpack_heads.2 = (bf16[128,2048]{1,0:T(8,128)(2,1)}, bf16[128,2048]{1,0:T(8,128)(2,1)}) custom-call(bf16[8,4,128,128]{3,2,1,0:T(8,128)(2,1)S(1)} %all-to-all-done.2.array), custom_call_target="tpu_custom_call" | custom-call | tf_op jit(solution)/shard_map/unpack_heads/pallas_call | solution.py:231
  75.9 8.4 %all-to-all-done.3.array = bf16[8,2,128,128]{3,2,1,0:T(8,128)(2,1)S(1)} async-done(((bf16[8,2,128,128]{3,2,1,0:T(8,128)(2,1)}), bf16[8,2,128,128]{3,2,1,0:T(8,128)(2,1)S(1)}, u32[]{:S(2)}, u32[]{:S(2)}) %all-to-all-start.3) | async-done | bytes 524320 | tf_op jit(solution)/shard_map/all_to_all | solution.py:31
  84.2 0.9 %unpack_heads.3 = (bf16[128,1024]{1,0:T(8,128)(2,1)}, bf16[128,1024]{1,0:T(8,128)(2,1)}) custom-call(bf16[8,2,128,128]{3,2,1,0:T(8,128)(2,1)S(1)} %all-to-all-done.3.array), custom_call_target="tpu_custom_call" | custom-call | tf_op jit(solution)/shard_map/unpack_heads/pallas_call | solution.py:231
  (4 shorter events, 0.0 us)
Async XLA Ops:
  2.5 6.9 %copy-start = (bf16[128,2048]{1,0:T(8,128)(2,1)S(1)}, bf16[128,2048]{1,0:T(8,128)(2,1)}, u32[]{:S(2)}) copy-start(bf16[128,2048]{1,0:T(8,128)(2,1)} %first.1) | copy-start | bytes 1572868
  2.5 7.0 %copy-start.1 = (bf16[128,2048]{1,0:T(8,128)(2,1)S(1)}, bf16[128,2048]{1,0:T(8,128)(2,1)}, u32[]{:S(2)}) copy-start(bf16[128,2048]{1,0:T(8,128)(2,1)} %second.1) | copy-start | bytes 1572868
  2.6 15.1 %all-to-all-start.1 = ((bf16[8,2,128,128]{3,2,1,0:T(8,128)(2,1)}), bf16[8,2,128,128]{3,2,1,0:T(8,128)(2,1)S(1)}, u32[]{:S(2)}, u32[]{:S(2)}) async-start(bf16[8,2,128,128]{3,2,1,0:T(8,128)(2,1)} %pack_heads.3), calls=%async_computation.1 | async-start | bytes 1048576 | tf_op jit(solution)/shard_map/all_to_all | solution.py:31
  8.1 0.7 copy-start.2
  17.7 18.2 %all-to-all-start = ((bf16[8,4,128,128]{3,2,1,0:T(8,128)(2,1)}), bf16[8,4,128,128]{3,2,1,0:T(8,128)(2,1)S(1)}, u32[]{:S(2)}, u32[]{:S(2)}) async-start(bf16[8,4,128,128]{3,2,1,0:T(8,128)(2,1)} %pack_heads.2), calls=%async_computation | async-start | bytes 2097152 | tf_op jit(solution)/shard_map/all_to_all | solution.py:31
  21.2 14.7 %collective-permute-start = (bf16[8,2,128,128]{3,2,1,0:T(8,128)(2,1)S(1)}, bf16[8,2,128,128]{3,2,1,0:T(8,128)(2,1)S(1)}, u32[]{:S(2)}, u32[]{:S(2)}) collective-permute-start(bf16[8,2,128,128]{3,2,1,0:T(8,128)(2,1)S(1)} %all-to-all-done.1.kv), channel_id=1, source_target_pairs={{0,12},{12,16},{1,13},{13,17},{2,14},{14,18},{3,15},{15,19},{4,8},... | collective-permute-start | bytes 1572872 | tf_op jit(solution)/shard_map/ppermute | solution.py:267
  43.6 20.2 %collective-permute-start.1 = (bf16[8,2,128,128]{3,2,1,0:T(8,128)(2,1)}, bf16[8,2,128,128]{3,2,1,0:T(8,128)(2,1)S(1)}, u32[]{:S(2)}, u32[]{:S(2)}) collective-permute-start(bf16[8,2,128,128]{3,2,1,0:T(8,128)(2,1)} %get-tuple-element.23), channel_id=1, source_target_pairs={{12,0},{16,12},{13,1},{17,13},{14,2},{18,14},{15,3},{19,15},{8,4},... | collective-permute-start | bytes 1572872 | tf_op jit(solution)/shard_map/ppermute | solution.py:271
  51.1 19.9 %all-to-all-start.2 = ((bf16[8,4,128,128]{3,2,1,0:T(8,128)(2,1)}), bf16[8,4,128,128]{3,2,1,0:T(8,128)(2,1)S(1)}, u32[]{:S(2)}, u32[]{:S(2)}) async-start(bf16[8,4,128,128]{3,2,1,0:T(8,128)(2,1)} %get-tuple-element.19), calls=%async_computation.2 | async-start | bytes 2097152 | tf_op jit(solution)/shard_map/all_to_all | solution.py:31
  71.0 13.3 %all-to-all-start.3 = ((bf16[8,2,128,128]{3,2,1,0:T(8,128)(2,1)}), bf16[8,2,128,128]{3,2,1,0:T(8,128)(2,1)S(1)}, u32[]{:S(2)}, u32[]{:S(2)}) async-start(bf16[8,2,128,128]{3,2,1,0:T(8,128)(2,1)} %join_grads.1), calls=%async_computation.3 | async-start | bytes 1048576 | tf_op jit(solution)/shard_map/all_to_all | solution.py:31

commit v6 on v5

--- a/solution.py
+++ b/solution.py
@@ -67,14 +67,17 @@
     def halo_at(block):
         return lax.rem(block + (1 - half) * (HALF_BLKS // 2), HALF_BLKS) * PAIR
 
-    for block in range(HALF_BLKS):
-        for ref, at, first in ((halo, halo_at, 0), (kv, own_at, HALF_BLKS)):
-            k_blk = ref[pl.ds(at(block), PAIR), 0].reshape(BLK, HD)
-            v_blk = ref[pl.ds(at(block), PAIR), 1].reshape(BLK, HD)
-            k_rows[first + block] = k_blk
-            v_rows[first + block] = v_blk
-            k_cols[first + block] = k_blk.T
-            v_cols[first + block] = v_blk.T
+    def prepare(ref, at, place):
+        k_blk = ref[pl.ds(at, PAIR), 0].reshape(BLK, HD)
+        v_blk = ref[pl.ds(at, PAIR), 1].reshape(BLK, HD)
+        k_rows[place] = k_blk
+        v_rows[place] = v_blk
+        k_cols[place] = k_blk.T
+        v_cols[place] = v_blk.T
+
+    for block in range(HALF_BLKS):
+        prepare(kv, own_at(block), HALF_BLKS + block)
+        pl.when(block >= info[1])(lambda block=block: prepare(halo, halo_at(block), block))
     for sums in (key_grads, value_grads):
         sums[:HALF_BLKS] = jnp.zeros((HALF_BLKS, BLK, HD), jnp.float32)
 
@@ -148,8 +151,8 @@
     halo_copy.start()
     for block in range(HALF_BLKS):
         at_pair = pl.ds(own_at(block), PAIR)
-        own_grads[at_pair, 0] = (key_grads[HALF_BLKS + block] * q_scale).astype(jnp.bfloat16).reshape(PAIR, TOK, HD)
-        own_grads[at_pair, 1] = value_grads[HALF_BLKS + block].astype(jnp.bfloat16).reshape(PAIR, TOK, HD)
+        own_grads[at_pair, 0] = (key_grads[HALF_BLKS + block] * q_scale).reshape(PAIR, TOK, HD)
+        own_grads[at_pair, 1] = value_grads[HALF_BLKS + block].reshape(PAIR, TOK, HD)
     for block in range(HALF_BLKS):
         od_copy(block).wait()
     halo_copy.wait()
@@ -162,7 +165,7 @@
         attend_kernel,
         out_shape=(
             pltpu.HBM((PEERS, 2 * GROUP, TOK, HD), jnp.bfloat16),
-            jax.ShapeDtypeStruct((PEERS, 2, TOK, HD), jnp.bfloat16),
+            jax.ShapeDtypeStruct((PEERS, 2, TOK, HD), jnp.float32),
             pltpu.HBM((PEERS, 2, TOK, HD), jnp.bfloat16),
         ),
         in_specs=[pl.BlockSpec(memory_space=pltpu.SMEM)] + [in_vmem] * 4,
@@ -239,7 +242,7 @@
 
 
 def join_kernel(own, back, out):
-    out[...] = (own[...].astype(jnp.float32) + back[...].astype(jnp.float32)).astype(jnp.bfloat16)
+    out[...] = (own[...] + back[...].astype(jnp.float32)).astype(jnp.bfloat16)
 
 
 def joined(own, back):

time: 85.2 us -> 85.4 us (level)
  Pallas kernels: 13.8 us -> 14.8 us
    pallas_call x1, Pallas kernels: 7.65 us -> 8.66 us  [attend_half(): pl.pallas_call(attend_kernel, out_shape=(pltpu.HBM((PEERS, 2 * GROUP, TOK...]
where the time goes in v6:
time: 85.4 us
  waiting for transfers between devices  40.7 us (48%)
  starting transfers between devices  27.7 us (32%)
  Pallas kernels  14.8 us (17%)
    all_to_all x4, waiting for transfers between devices, exchange(): lax.all_to_all(array, 'ctx', split_axis=0, concat_axis=0, tiled=True, axi...  33 us
    all_to_all x4, starting transfers between devices, exchange(): lax.all_to_all(array, 'ctx', split_axis=0, concat_axis=0, tiled=True, axi...  17.1 us
    pallas_call x1, Pallas kernels, attend_half(): pl.pallas_call(attend_kernel, out_shape=(pltpu.HBM((PEERS, 2 * GROUP, TOK...  8.66 us
    ppermute x1, waiting for transfers between devices, on_device(): back = lax.ppermute(halo_grads, both, behind)  7.69 us
    ppermute x1, starting transfers between devices, on_device(): back = lax.ppermute(halo_grads, both, behind)  6.62 us
    ppermute x1, starting transfers between devices, on_device(): halo = lax.ppermute(kv, both, ahead)  4 us
    pallas_call x2, Pallas kernels, packed(): pl.pallas_call(functools.partial(pack_kernel, width), out_shape=jax.Shape...  3.07 us
    pallas_call x2, Pallas kernels, unpacked(): pl.pallas_call(functools.partial(unpack_kernel, width), out_shape=(rows,...  2.19 us
  transfers between devices with their start and end apart: 6, of which 6 were waited for; matrix products, arithmetic and copies ran while one was open for 1% of the time, Pallas kernels for 4%

profile of v6, /device:TPU:384, one launch (start us, length us, event | category | flops | bytes accessed | tf_op | source)
XLA Modules:
  0.0 85.4 jit_solution(16058096535399626984)
XLA Ops:
  0.6 1.9 %pack_heads.3 = bf16[8,2,128,128]{3,2,1,0:T(8,128)(2,1)} custom-call(bf16[128,1024]{1,0:T(8,128)(2,1)} %first.2, bf16[128,1024]{1,0:T(8,128)(2,1)} %second.2), custom_call_target="tpu_custom_call" | custom-call | tf_op jit(solution)/shard_map/pack_heads/pallas_call | solution.py:215
  2.5 0.0 copy-start
  2.5 0.0 copy-start.1
  2.6 5.5 %all-to-all-start.1 = ((bf16[8,2,128,128]{3,2,1,0:T(8,128)(2,1)}), bf16[8,2,128,128]{3,2,1,0:T(8,128)(2,1)S(1)}, u32[]{:S(2)}, u32[]{:S(2)}) async-start(bf16[8,2,128,128]{3,2,1,0:T(8,128)(2,1)} %pack_heads.3), calls=%async_computation.1 | async-start | bytes 1048576 | tf_op jit(solution)/shard_map/all_to_all | solution.py:31
  8.1 0.0 copy-start.2
  8.1 0.6 copy-done.2
  8.7 0.1 select_reduce_fusion.1
  8.8 0.4 select_reduce_fusion
  9.2 0.2 slice_reduce_fusion
  9.4 0.1 pad_add_fusion.1.info
  9.5 0.0 copy-done
  9.5 0.0 copy-done.1
  9.5 1.2 %pack_heads.2 = bf16[8,4,128,128]{3,2,1,0:T(8,128)(2,1)} custom-call(bf16[128,2048]{1,0:T(8,128)(2,1)S(1)} %copy-done, bf16[128,2048]{1,0:T(8,128)(2,1)S(1)} %copy-done.1), custom_call_target="tpu_custom_call" | custom-call | tf_op jit(solution)/shard_map/pack_heads/pallas_call | solution.py:215
  10.7 7.0 %all-to-all-done.1.kv = bf16[8,2,128,128]{3,2,1,0:T(8,128)(2,1)S(1)} async-done(((bf16[8,2,128,128]{3,2,1,0:T(8,128)(2,1)}), bf16[8,2,128,128]{3,2,1,0:T(8,128)(2,1)S(1)}, u32[]{:S(2)}, u32[]{:S(2)}) %all-to-all-start.1) | async-done | bytes 524320 | tf_op jit(solution)/shard_map/all_to_all | solution.py:31
  17.7 3.6 %all-to-all-start = ((bf16[8,4,128,128]{3,2,1,0:T(8,128)(2,1)}), bf16[8,4,128,128]{3,2,1,0:T(8,128)(2,1)S(1)}, u32[]{:S(2)}, u32[]{:S(2)}) async-start(bf16[8,4,128,128]{3,2,1,0:T(8,128)(2,1)} %pack_heads.2), calls=%async_computation | async-start | bytes 2097152 | tf_op jit(solution)/shard_map/all_to_all | solution.py:31
  21.2 4.0 %collective-permute-start = (bf16[8,2,128,128]{3,2,1,0:T(8,128)(2,1)S(1)}, bf16[8,2,128,128]{3,2,1,0:T(8,128)(2,1)S(1)}, u32[]{:S(2)}, u32[]{:S(2)}) collective-permute-start(bf16[8,2,128,128]{3,2,1,0:T(8,128)(2,1)S(1)} %all-to-all-done.1.kv), channel_id=1, source_target_pairs={{0,12},{12,16},{1,13},{13,17},{2,14},{14,18},{3,15},{15,19},{4,8},... | collective-permute-start | bytes 1572872 | tf_op jit(solution)/shard_map/ppermute | solution.py:270
  25.2 10.6 %all-to-all-done.qd = bf16[8,4,128,128]{3,2,1,0:T(8,128)(2,1)S(1)} async-done(((bf16[8,4,128,128]{3,2,1,0:T(8,128)(2,1)}), bf16[8,4,128,128]{3,2,1,0:T(8,128)(2,1)S(1)}, u32[]{:S(2)}, u32[]{:S(2)}) %all-to-all-start) | async-done | bytes 1048608 | tf_op jit(solution)/shard_map/all_to_all | solution.py:31
  35.9 0.1 collective-permute-done.halo
  36.0 8.7 %attend_half.1 = (bf16[8,4,128,128]{3,2,1,0:T(8,128)(2,1)}, f32[8,2,128,128]{3,2,1,0:T(8,128)S(1)}, bf16[8,2,128,128]{3,2,1,0:T(8,128)(2,1)}) custom-call(s32[5]{0:T(128)S(1)} %pad_add_fusion.1.info, bf16[8,4,128,128]{3,2,1,0:T(8,128)(2,1)S(1)} %all-to-all-done.qd, bf16[8,2,128,128]{3,2,1,0:T(8,128)(2,1)S(1)} %all-to-all-done.1.kv, ...), custom_call_target="tpu_custom_call" | custom-call | tf_op jit(solution)/shard_map/attend_half/pallas_call | solution.py:164
  44.6 6.6 %collective-permute-start.1 = (bf16[8,2,128,128]{3,2,1,0:T(8,128)(2,1)}, bf16[8,2,128,128]{3,2,1,0:T(8,128)(2,1)S(1)}, u32[]{:S(2)}, u32[]{:S(2)}) collective-permute-start(bf16[8,2,128,128]{3,2,1,0:T(8,128)(2,1)} %get-tuple-element.23), channel_id=1, source_target_pairs={{12,0},{16,12},{13,1},{17,13},{14,2},{18,14},{15,3},{19,15},{8,4},... | collective-permute-start | bytes 1572872 | tf_op jit(solution)/shard_map/ppermute | solution.py:274
  51.3 4.4 %all-to-all-start.2 = ((bf16[8,4,128,128]{3,2,1,0:T(8,128)(2,1)}), bf16[8,4,128,128]{3,2,1,0:T(8,128)(2,1)S(1)}, u32[]{:S(2)}, u32[]{:S(2)}) async-start(bf16[8,4,128,128]{3,2,1,0:T(8,128)(2,1)} %get-tuple-element.19), calls=%async_computation.2 | async-start | bytes 2097152 | tf_op jit(solution)/shard_map/all_to_all | solution.py:31
  55.6 7.7 %collective-permute-done.1.back = bf16[8,2,128,128]{3,2,1,0:T(8,128)(2,1)S(1)} collective-permute-done((bf16[8,2,128,128]{3,2,1,0:T(8,128)(2,1)}, bf16[8,2,128,128]{3,2,1,0:T(8,128)(2,1)S(1)}, u32[]{:S(2)}, u32[]{:S(2)}) %collective-permute-start.1) | collective-permute-done | bytes 524320 | tf_op jit(solution)/shard_map/ppermute | solution.py:274
  63.3 0.9 %join_grads.1 = bf16[8,2,128,128]{3,2,1,0:T(8,128)(2,1)} custom-call(f32[8,2,128,128]{3,2,1,0:T(8,128)S(1)} %get-tuple-element.22.own, bf16[8,2,128,128]{3,2,1,0:T(8,128)(2,1)S(1)} %collective-permute-done.1.back), custom_call_target="tpu_custom_call" | custom-call | flops 30000001024 | bytes 100000000 | tf_op jit(solution)/shard_map/join_grads/pallas_call | solution.py:250
  64.2 6.9 %all-to-all-done.2.array = bf16[8,4,128,128]{3,2,1,0:T(8,128)(2,1)S(1)} async-done(((bf16[8,4,128,128]{3,2,1,0:T(8,128)(2,1)}), bf16[8,4,128,128]{3,2,1,0:T(8,128)(2,1)S(1)}, u32[]{:S(2)}, u32[]{:S(2)}) %all-to-all-start.2) | async-done | bytes 1048608 | tf_op jit(solution)/shard_map/all_to_all | solution.py:31
  71.1 3.6 %all-to-all-start.3 = ((bf16[8,2,128,128]{3,2,1,0:T(8,128)(2,1)}), bf16[8,2,128,128]{3,2,1,0:T(8,128)(2,1)S(1)}, u32[]{:S(2)}, u32[]{:S(2)}) async-start(bf16[8,2,128,128]{3,2,1,0:T(8,128)(2,1)} %join_grads.1), calls=%async_computation.3 | async-start | bytes 1048576 | tf_op jit(solution)/shard_map/all_to_all | solution.py:31
  74.8 1.3 %unpack_heads.2 = (bf16[128,2048]{1,0:T(8,128)(2,1)}, bf16[128,2048]{1,0:T(8,128)(2,1)}) custom-call(bf16[8,4,128,128]{3,2,1,0:T(8,128)(2,1)S(1)} %all-to-all-done.2.array), custom_call_target="tpu_custom_call" | custom-call | tf_op jit(solution)/shard_map/unpack_heads/pallas_call | solution.py:234
  76.0 8.4 %all-to-all-done.3.array = bf16[8,2,128,128]{3,2,1,0:T(8,128)(2,1)S(1)} async-done(((bf16[8,2,128,128]{3,2,1,0:T(8,128)(2,1)}), bf16[8,2,128,128]{3,2,1,0:T(8,128)(2,1)S(1)}, u32[]{:S(2)}, u32[]{:S(2)}) %all-to-all-start.3) | async-done | bytes 524320 | tf_op jit(solution)/shard_map/all_to_all | solution.py:31
  84.4 0.9 %unpack_heads.3 = (bf16[128,1024]{1,0:T(8,128)(2,1)}, bf16[128,1024]{1,0:T(8,128)(2,1)}) custom-call(bf16[8,2,128,128]{3,2,1,0:T(8,128)(2,1)S(1)} %all-to-all-done.3.array), custom_call_target="tpu_custom_call" | custom-call | tf_op jit(solution)/shard_map/unpack_heads/pallas_call | solution.py:234
  (4 shorter events, 0.0 us)
Async XLA Ops:
  2.5 6.9 %copy-start = (bf16[128,2048]{1,0:T(8,128)(2,1)S(1)}, bf16[128,2048]{1,0:T(8,128)(2,1)}, u32[]{:S(2)}) copy-start(bf16[128,2048]{1,0:T(8,128)(2,1)} %first.1) | copy-start | bytes 1572868
  2.5 7.0 %copy-start.1 = (bf16[128,2048]{1,0:T(8,128)(2,1)S(1)}, bf16[128,2048]{1,0:T(8,128)(2,1)}, u32[]{:S(2)}) copy-start(bf16[128,2048]{1,0:T(8,128)(2,1)} %second.1) | copy-start | bytes 1572868
  2.6 15.1 %all-to-all-start.1 = ((bf16[8,2,128,128]{3,2,1,0:T(8,128)(2,1)}), bf16[8,2,128,128]{3,2,1,0:T(8,128)(2,1)S(1)}, u32[]{:S(2)}, u32[]{:S(2)}) async-start(bf16[8,2,128,128]{3,2,1,0:T(8,128)(2,1)} %pack_heads.3), calls=%async_computation.1 | async-start | bytes 1048576 | tf_op jit(solution)/shard_map/all_to_all | solution.py:31
  8.1 0.7 copy-start.2
  17.7 18.2 %all-to-all-start = ((bf16[8,4,128,128]{3,2,1,0:T(8,128)(2,1)}), bf16[8,4,128,128]{3,2,1,0:T(8,128)(2,1)S(1)}, u32[]{:S(2)}, u32[]{:S(2)}) async-start(bf16[8,4,128,128]{3,2,1,0:T(8,128)(2,1)} %pack_heads.2), calls=%async_computation | async-start | bytes 2097152 | tf_op jit(solution)/shard_map/all_to_all | solution.py:31
  21.2 14.7 %collective-permute-start = (bf16[8,2,128,128]{3,2,1,0:T(8,128)(2,1)S(1)}, bf16[8,2,128,128]{3,2,1,0:T(8,128)(2,1)S(1)}, u32[]{:S(2)}, u32[]{:S(2)}) collective-permute-start(bf16[8,2,128,128]{3,2,1,0:T(8,128)(2,1)S(1)} %all-to-all-done.1.kv), channel_id=1, source_target_pairs={{0,12},{12,16},{1,13},{13,17},{2,14},{14,18},{3,15},{15,19},{4,8},... | collective-permute-start | bytes 1572872 | tf_op jit(solution)/shard_map/ppermute | solution.py:270
  44.6 18.7 %collective-permute-start.1 = (bf16[8,2,128,128]{3,2,1,0:T(8,128)(2,1)}, bf16[8,2,128,128]{3,2,1,0:T(8,128)(2,1)S(1)}, u32[]{:S(2)}, u32[]{:S(2)}) collective-permute-start(bf16[8,2,128,128]{3,2,1,0:T(8,128)(2,1)} %get-tuple-element.23), channel_id=1, source_target_pairs={{12,0},{16,12},{13,1},{17,13},{14,2},{18,14},{15,3},{19,15},{8,4},... | collective-permute-start | bytes 1572872 | tf_op jit(solution)/shard_map/ppermute | solution.py:274
  51.3 19.9 %all-to-all-start.2 = ((bf16[8,4,128,128]{3,2,1,0:T(8,128)(2,1)}), bf16[8,4,128,128]{3,2,1,0:T(8,128)(2,1)S(1)}, u32[]{:S(2)}, u32[]{:S(2)}) async-start(bf16[8,4,128,128]{3,2,1,0:T(8,128)(2,1)} %get-tuple-element.19), calls=%async_computation.2 | async-start | bytes 2097152 | tf_op jit(solution)/shard_map/all_to_all | solution.py:31
  71.1 13.3 %all-to-all-start.3 = ((bf16[8,2,128,128]{3,2,1,0:T(8,128)(2,1)}), bf16[8,2,128,128]{3,2,1,0:T(8,128)(2,1)S(1)}, u32[]{:S(2)}, u32[]{:S(2)}) async-start(bf16[8,2,128,128]{3,2,1,0:T(8,128)(2,1)} %join_grads.1), calls=%async_computation.3 | async-start | bytes 1048576 | tf_op jit(solution)/shard_map/all_to_all | solution.py:31
